TPU v7x, 256 devices: a whole 4x4x8 slice. The times are simulated.
256 devices in a mesh: section: 8 (over x, core), dp: 32 (over z, y).
Axes of the slice: x: 4, y: 4, z: 8, core: 2. Of those that a mesh axis runs over, the one named last changes fastest.
Arguments:
- saved_inputs: bfloat16 [8, 32, 4, 32, 4096], P('section', 'dp'), may hold values from -6 to 6
- saved_queries: bfloat16 [8, 32, 4, 32, 4096], P('section', 'dp'), may hold values from -6 to 6
- norm_gain: float32 [8, 4096], P('section'), may hold values from 0.1 to 1.9
- key_weight: bfloat16 [8, 4096, 512], P('section'), may hold values from -0.09375 to 0.09375
- value_weight: bfloat16 [8, 4096, 512], P('section'), may hold values from -0.09375 to 0.09375
- out_cotangent: bfloat16 [32, 4, 32, 4096], P('dp'), may hold values from -6 to 6
- token_counts: int32 [32, 4], P('dp'), may hold values from 8 to 32
- segment_ids: int32 [32, 4, 32], P('dp'), may hold values from 0 to 3, never falling along the last dimension, each value on 1 to 16 neighbouring positions
Outputs:
- input_grads: bfloat16 [8, 32, 4, 32, 4096], P('section', 'dp')
- key_weight_grad: float32 [8, 4096, 512], P('section', 'dp')
- value_weight_grad: float32 [8, 4096, 512], P('section', 'dp')
- gain_grad: float32 [8, 4096], P('section')
Inputs may be any that keep to these rules, and one draw needn't show every extreme that they name: `segment_ids`: within each micro-batch the segment ids never fall.
All inputs are finite; a program needn't handle non-finite values.
Results may differ from a plain program's by a relative error of at most 0.034.
Values may be sent and summed in bfloat16 or wider, within the bound.
A program may use at most 128 MiB of HBM per device.

v0:
```python
import jax
import jax.numpy as jnp
from jax import lax
from jax.sharding import PartitionSpec as P

HD = 128
HEADS = 32
KVH = 4


EPS = 1e-05


def shifted(value, axis, steps):
    count = lax.axis_size(axis)
    initial, last = (max(0, -steps), min(count, count - steps))
    return lax.ppermute(value, axis, [(source, source + steps) for source in range(initial, last)])


def normalize(features, gain_row):
    inverse = lax.rsqrt(jnp.mean(features * features, axis=-1, keepdims=True) + EPS)
    return features * inverse * gain_row


def layer_pieces(inputs, queries, gain_row, key_mat, value_mat, out_grad, count, segments):
    row_count = inputs.shape[0]
    group_heads = HEADS // KVH
    kv_cols = key_mat.shape[1]
    normed_f32, norm_pull = jax.vjp(normalize, inputs.astype(jnp.float32), gain_row)
    normed = normed_f32.astype(jnp.bfloat16)
    keys = jnp.dot(normed, key_mat, preferred_element_type=jnp.float32).astype(jnp.bfloat16)
    values = jnp.dot(normed, value_mat, preferred_element_type=jnp.float32).astype(jnp.bfloat16)
    positions = jnp.arange(row_count, dtype=jnp.int32)
    is_valid = positions < count
    allowed = (positions[None, :] <= positions[:, None]) & (
        segments[None, :] == segments[:, None]
    ) & is_valid[None, :] | (positions[None, :] == positions[:, None])
    query_heads = queries.reshape(row_count, KVH, group_heads, HD)
    key_heads = keys.reshape(row_count, KVH, HD)
    value_heads = values.reshape(row_count, KVH, HD)
    score_scale = HD ** (-0.5)
    scores = (
        jnp.einsum("igad,jgd->gaij", query_heads, key_heads, preferred_element_type=jnp.float32)
        * score_scale
    )
    weights = jnp.where(allowed, jnp.exp(scores), 0.0)
    probabilities = weights / jnp.sum(weights, axis=-1, keepdims=True)
    probs_low = probabilities.astype(jnp.bfloat16)
    head_grad = jnp.where(is_valid[:, None], out_grad, jnp.zeros_like(out_grad)).reshape(
        row_count, KVH, group_heads, HD
    )
    value_grad = (
        jnp.einsum("gaij,igad->jgd", probs_low, head_grad, preferred_element_type=jnp.float32)
        .astype(jnp.bfloat16)
        .reshape(row_count, kv_cols)
    )
    prob_grad = jnp.einsum(
        "igad,jgd->gaij", head_grad, value_heads, preferred_element_type=jnp.float32
    )
    score_grad = (
        probabilities
        * (prob_grad - jnp.sum(probabilities * prob_grad, axis=-1, keepdims=True))
        * score_scale
    )
    score_low = score_grad.astype(jnp.bfloat16)
    key_grad = (
        jnp.einsum("gaij,igad->jgd", score_low, query_heads, preferred_element_type=jnp.float32)
        .astype(jnp.bfloat16)
        .reshape(row_count, kv_cols)
    )
    normed_grad = jnp.einsum(
        "rk,dk->rd", key_grad, key_mat, preferred_element_type=jnp.float32
    ) + jnp.einsum("rk,dk->rd", value_grad, value_mat, preferred_element_type=jnp.float32)
    input_pull, gain_term = norm_pull(normed_grad)
    in_grad = (out_grad.astype(jnp.float32) + input_pull).astype(jnp.bfloat16)
    both_grads = jnp.concatenate([key_grad, value_grad], axis=1)
    return (in_grad, normed, both_grads, gain_term)


def shards(
    saved_inputs,
    saved_queries,
    norm_gain,
    key_weight,
    value_weight,
    out_cotangent,
    token_counts,
    segment_ids,
):
    input_all = saved_inputs[0, 0]
    query_all = saved_queries[0, 0]
    gain_row = norm_gain[0]
    key_mat = key_weight[0]
    value_mat = value_weight[0]
    cotangent = out_cotangent[0]
    counts = token_counts[0]
    segments_all = segment_ids[0]
    micro_count, row_count, model_width = input_all.shape
    kv_cols = key_mat.shape[1]
    sections = lax.axis_size("section")
    section_id = lax.axis_index("section")
    is_last = section_id == sections - 1
    stores = (
        jnp.zeros_like(input_all),
        jnp.zeros((micro_count, row_count, 2 * kv_cols), jnp.bfloat16),
    )

    def advance(step_id, state_carry):
        incoming, grads_out, gain_total, stores = state_carry
        micro_id = step_id - (sections - 1 - section_id)
        active = (micro_id >= 0) & (micro_id < micro_count)
        slot_pick = jnp.clip(micro_id, 0, micro_count - 1)
        out_grad = jnp.where(is_last, cotangent[slot_pick], incoming)
        in_grad, normed, both_grads, gain_term = layer_pieces(
            input_all[slot_pick],
            query_all[slot_pick],
            gain_row,
            key_mat,
            value_mat,
            out_grad,
            counts[slot_pick],
            segments_all[slot_pick],
        )
        grads_out = grads_out.at[slot_pick].set(jnp.where(active, in_grad, grads_out[slot_pick]))
        gain_total = gain_total + jnp.where(active, gain_term, 0.0)
        saved_normed, saved_grads = stores
        saved_normed = saved_normed.at[slot_pick].set(
            jnp.where(active, normed, saved_normed[slot_pick])
        )
        saved_grads = saved_grads.at[slot_pick].set(
            jnp.where(active, both_grads, saved_grads[slot_pick])
        )
        stores = (saved_normed, saved_grads)
        incoming = shifted(in_grad, "section", -1)
        return (incoming, grads_out, gain_total, stores)

    initial = (
        jnp.zeros((row_count, model_width), jnp.bfloat16),
        jnp.zeros_like(input_all),
        jnp.zeros((model_width,), jnp.float32),
        stores,
    )
    incoming, grads_out, gain_total, stores = lax.fori_loop(
        0, sections + micro_count - 1, advance, initial
    )
    saved_normed, saved_grads = stores
    grad_term = jnp.einsum(
        "mrd,mrk->dk", saved_normed, saved_grads, preferred_element_type=jnp.float32
    )
    summed = lax.psum_scatter(
        grad_term.astype(jnp.bfloat16), "dp", scatter_dimension=0, tiled=True
    ).astype(jnp.float32)
    gain_sum = lax.psum(gain_total, "dp")
    key_out = summed[:, :kv_cols][None]
    value_out = summed[:, kv_cols:][None]
    return (grads_out[None, None], key_out, value_out, gain_sum[None])


def solution(mesh):
    placed = (
        P("section", "dp", None, None, None),
        P("section", "dp", None, None, None),
        P("section", None),
        P("section", None, None),
        P("section", None, None),
        P("dp", None, None, None),
        P("dp", None),
        P("dp", None, None),
    )
    return jax.shard_map(
        shards,
        mesh=mesh,
        in_specs=placed,
        out_specs=(
            P("section", "dp", None, None, None),
            P("section", "dp", None),
            P("section", "dp", None),
            P("section", None),
        ),
        check_vma=False,
    )
```

profile of v0, /device:TPU:32, one launch (start us, length us, event | category | flops | bytes accessed | tf_op | source)
XLA Modules:
  0.0 609.5 jit_solution(4149062896187535595)
XLA Ops:
  9.5 349.4 %while.27 = (s32[]{:T(128)}, bf16[32,4096]{1,0:T(8,128)(2,1)S(1)}, bf16[4,32,4096]{2,1,0:T(8,128)(2,1)}, f32[4096]{0:T(1024)S(1)}, bf16[4,32,4096]{2,1,0:T(8,128...) while((s32[]{:T(128)}, bf16[32,4096]{1,0:T(8,128)(2,1)S(1)}, ...), condition=%wide.region_7.8_spmd.clone, body=%wide.region_0.7_spmd.clone.sunk | while | flops 576076096 | bytes 50238584 | solution.py:143
  13.2 3.2 convolution_convert_fusion.5
  16.5 3.1 convolution_convert_fusion.4
  25.4 3.7 fusion.113
  41.2 3.2 convolution_convert_fusion.5
  44.4 3.1 convolution_convert_fusion.4
  53.4 3.7 fusion.113
  64.0 5.0 collective-permute-done
  72.8 3.2 convolution_convert_fusion.5
  76.0 3.1 convolution_convert_fusion.4
  84.9 3.7 fusion.113
  95.6 5.7 collective-permute-done
  105.0 3.2 convolution_convert_fusion.5
  108.2 3.1 convolution_convert_fusion.4
  117.2 3.7 fusion.113
  127.8 5.7 collective-permute-done
  137.2 3.2 convolution_convert_fusion.5
  140.4 3.1 convolution_convert_fusion.4
  149.4 3.7 fusion.113
  160.0 5.7 collective-permute-done
  169.4 3.2 convolution_convert_fusion.5
  172.6 3.1 convolution_convert_fusion.4
  181.6 3.7 fusion.113
  192.2 5.7 collective-permute-done
  201.6 3.2 convolution_convert_fusion.5
  204.8 3.1 convolution_convert_fusion.4
  213.8 3.7 fusion.113
  224.4 5.7 collective-permute-done
  233.8 3.2 convolution_convert_fusion.5
  237.0 3.1 convolution_convert_fusion.4
  246.0 3.7 fusion.113
  256.6 5.7 collective-permute-done
  266.0 3.2 convolution_convert_fusion.5
  269.2 3.1 convolution_convert_fusion.4
  278.2 3.7 fusion.113
  288.8 5.7 collective-permute-done
  298.2 3.2 convolution_convert_fusion.5
  301.5 3.1 convolution_convert_fusion.4
  310.4 3.7 fusion.113
  316.3 2.8 fusion.117
  321.1 5.7 collective-permute-done
  330.5 3.2 convolution_convert_fusion.5
  333.7 3.1 convolution_convert_fusion.4
  342.6 3.7 fusion.113
  353.3 5.7 collective-permute-done
  359.0 6.8 %bitcast_convert_fusion = bf16[4096,1024]{1,0:T(8,128)(2,1)} fusion(bf16[4,32,4096]{2,1,0:T(8,128)(2,1)} %get-tuple-element.433, bf16[4,32,1024]{2,1,0:T(8,128)(2,1)S(1)} %get-tuple-element.434), kind=kOutput, calls=%fused_computation.73 | convolution fusion | flops 1077936128 | bytes 9699328 | tf_op jit(solution)/shard_map/mrd,mrk->dk/dot_general | solution.py:147
  365.8 139.9 %psum.7 = f32[1,4096]{1,0:T(1,128)} all-reduce(f32[1,4096]{1,0:T(1,128)S(1)} %bitcast.204), channel_id=1, replica_groups=mesh['section'=8,'dp'=32] {'dp'}, use_global_device_ids=true, to_apply=%region_9.10 | all-reduce | flops 4096 | bytes 32768 | tf_op jit(solution)/shard_map/psum | solution.py:153
  505.7 95.1 %reduce-scatter.2.cloned.1.call-done = bf16[128,1024]{1,0:T(8,128)(2,1)} async-done(((bf16[4096,1024]{1,0:T(8,128)(2,1)}), bf16[128,1024]{1,0:T(8,128)(2,1)}) %reduce-scatter.2.cloned.1.call-update) | async-done | bytes 262160 | tf_op jit(solution)/shard_map/reduce_scatter | solution.py:150
  (449 shorter events, 183.7 us)
Async XLA Ops:
  7.2 593.6 %reduce-scatter.2.cloned.1.call-start = ((), (), s32[]{:S(2)}) async-start(), calls=%async_computation.1 | async-start | bytes 8650752 | tf_op jit(solution)/shard_map/reduce_scatter | solution.py:150
  9.5 6.9 %copy-start.1 = (bf16[4,32,4096]{2,1,0:T(8,128)(2,1)S(1)}, bf16[4,32,4096]{2,1,0:T(8,128)(2,1)}, u32[]{:S(2)}) copy-start(bf16[4,32,4096]{2,1,0:T(8,128)(2,1)} %get-tuple-element.698) | copy-start | bytes 3145732 | tf_op jit(solution)/shard_map/while
  9.5 6.9 %copy-start.2 = (f32[1,4096]{1,0:T(1,128)S(1)}, f32[1,4096]{1,0:T(1,128)}, u32[]{:S(2)}) copy-start(f32[1,4096]{1,0:T(1,128)} %get-tuple-element.699) | copy-start | bytes 49156 | tf_op jit(solution)/shard_map/while
  25.2 3.9 copy-start
  25.4 5.2 copy-start.3
  34.1 3.4 collective-permute-start
  37.5 6.9 %copy-start.1 = (bf16[4,32,4096]{2,1,0:T(8,128)(2,1)S(1)}, bf16[4,32,4096]{2,1,0:T(8,128)(2,1)}, u32[]{:S(2)}) copy-start(bf16[4,32,4096]{2,1,0:T(8,128)(2,1)} %get-tuple-element.698) | copy-start | bytes 3145732 | tf_op jit(solution)/shard_map/while
  37.5 6.9 %copy-start.2 = (f32[1,4096]{1,0:T(1,128)S(1)}, f32[1,4096]{1,0:T(1,128)}, u32[]{:S(2)}) copy-start(f32[1,4096]{1,0:T(1,128)} %get-tuple-element.699) | copy-start | bytes 49156 | tf_op jit(solution)/shard_map/while
  53.1 3.9 copy-start
  53.3 5.2 copy-start.3
  62.0 7.1 %collective-permute-start = (bf16[32,4096]{1,0:T(8,128)(2,1)S(1)}, bf16[32,4096]{1,0:T(8,128)(2,1)S(1)}, u32[]{:S(2)}, u32[]{:S(2)}) collective-permute-start(bf16[32,4096]{1,0:T(8,128)(2,1)S(1)} %get-tuple-element.638), channel_id=1, source_target_pairs={{32,0},{64,32},{96,64},{128,96},{160,128},{192,160},{224,192},{33,... | collective-permute-start | bytes 786440 | tf_op jit(solution)/shard_map/while/body/eval_jaxpr/ppermute | solution.py:17
  69.1 6.9 %copy-start.1 = (bf16[4,32,4096]{2,1,0:T(8,128)(2,1)S(1)}, bf16[4,32,4096]{2,1,0:T(8,128)(2,1)}, u32[]{:S(2)}) copy-start(bf16[4,32,4096]{2,1,0:T(8,128)(2,1)} %get-tuple-element.698) | copy-start | bytes 3145732 | tf_op jit(solution)/shard_map/while
  69.1 6.9 %copy-start.2 = (f32[1,4096]{1,0:T(1,128)S(1)}, f32[1,4096]{1,0:T(1,128)}, u32[]{:S(2)}) copy-start(f32[1,4096]{1,0:T(1,128)} %get-tuple-element.699) | copy-start | bytes 49156 | tf_op jit(solution)/shard_map/while
  84.7 3.9 copy-start
  84.9 5.2 copy-start.3
  93.6 7.7 %collective-permute-start = (bf16[32,4096]{1,0:T(8,128)(2,1)S(1)}, bf16[32,4096]{1,0:T(8,128)(2,1)S(1)}, u32[]{:S(2)}, u32[]{:S(2)}) collective-permute-start(bf16[32,4096]{1,0:T(8,128)(2,1)S(1)} %get-tuple-element.638), channel_id=1, source_target_pairs={{32,0},{64,32},{96,64},{128,96},{160,128},{192,160},{224,192},{33,... | collective-permute-start | bytes 786440 | tf_op jit(solution)/shard_map/while/body/eval_jaxpr/ppermute | solution.py:17
  101.3 6.9 %copy-start.1 = (bf16[4,32,4096]{2,1,0:T(8,128)(2,1)S(1)}, bf16[4,32,4096]{2,1,0:T(8,128)(2,1)}, u32[]{:S(2)}) copy-start(bf16[4,32,4096]{2,1,0:T(8,128)(2,1)} %get-tuple-element.698) | copy-start | bytes 3145732 | tf_op jit(solution)/shard_map/while
  101.3 6.9 %copy-start.2 = (f32[1,4096]{1,0:T(1,128)S(1)}, f32[1,4096]{1,0:T(1,128)}, u32[]{:S(2)}) copy-start(f32[1,4096]{1,0:T(1,128)} %get-tuple-element.699) | copy-start | bytes 49156 | tf_op jit(solution)/shard_map/while
  117.1 5.2 copy-start.3
  125.8 7.7 %collective-permute-start = (bf16[32,4096]{1,0:T(8,128)(2,1)S(1)}, bf16[32,4096]{1,0:T(8,128)(2,1)S(1)}, u32[]{:S(2)}, u32[]{:S(2)}) collective-permute-start(bf16[32,4096]{1,0:T(8,128)(2,1)S(1)} %get-tuple-element.638), channel_id=1, source_target_pairs={{32,0},{64,32},{96,64},{128,96},{160,128},{192,160},{224,192},{33,... | collective-permute-start | bytes 786440 | tf_op jit(solution)/shard_map/while/body/eval_jaxpr/ppermute | solution.py:17
  133.5 6.9 %copy-start.1 = (bf16[4,32,4096]{2,1,0:T(8,128)(2,1)S(1)}, bf16[4,32,4096]{2,1,0:T(8,128)(2,1)}, u32[]{:S(2)}) copy-start(bf16[4,32,4096]{2,1,0:T(8,128)(2,1)} %get-tuple-element.698) | copy-start | bytes 3145732 | tf_op jit(solution)/shard_map/while
  133.5 6.9 %copy-start.2 = (f32[1,4096]{1,0:T(1,128)S(1)}, f32[1,4096]{1,0:T(1,128)}, u32[]{:S(2)}) copy-start(f32[1,4096]{1,0:T(1,128)} %get-tuple-element.699) | copy-start | bytes 49156 | tf_op jit(solution)/shard_map/while
  149.4 5.2 copy-start.3
  158.0 7.7 %collective-permute-start = (bf16[32,4096]{1,0:T(8,128)(2,1)S(1)}, bf16[32,4096]{1,0:T(8,128)(2,1)S(1)}, u32[]{:S(2)}, u32[]{:S(2)}) collective-permute-start(bf16[32,4096]{1,0:T(8,128)(2,1)S(1)} %get-tuple-element.638), channel_id=1, source_target_pairs={{32,0},{64,32},{96,64},{128,96},{160,128},{192,160},{224,192},{33,... | collective-permute-start | bytes 786440 | tf_op jit(solution)/shard_map/while/body/eval_jaxpr/ppermute | solution.py:17
  165.7 6.9 %copy-start.1 = (bf16[4,32,4096]{2,1,0:T(8,128)(2,1)S(1)}, bf16[4,32,4096]{2,1,0:T(8,128)(2,1)}, u32[]{:S(2)}) copy-start(bf16[4,32,4096]{2,1,0:T(8,128)(2,1)} %get-tuple-element.698) | copy-start | bytes 3145732 | tf_op jit(solution)/shard_map/while
  165.7 6.9 %copy-start.2 = (f32[1,4096]{1,0:T(1,128)S(1)}, f32[1,4096]{1,0:T(1,128)}, u32[]{:S(2)}) copy-start(f32[1,4096]{1,0:T(1,128)} %get-tuple-element.699) | copy-start | bytes 49156 | tf_op jit(solution)/shard_map/while
  181.6 5.2 copy-start.3
  190.2 7.7 %collective-permute-start = (bf16[32,4096]{1,0:T(8,128)(2,1)S(1)}, bf16[32,4096]{1,0:T(8,128)(2,1)S(1)}, u32[]{:S(2)}, u32[]{:S(2)}) collective-permute-start(bf16[32,4096]{1,0:T(8,128)(2,1)S(1)} %get-tuple-element.638), channel_id=1, source_target_pairs={{32,0},{64,32},{96,64},{128,96},{160,128},{192,160},{224,192},{33,... | collective-permute-start | bytes 786440 | tf_op jit(solution)/shard_map/while/body/eval_jaxpr/ppermute | solution.py:17
  197.9 6.9 %copy-start.1 = (bf16[4,32,4096]{2,1,0:T(8,128)(2,1)S(1)}, bf16[4,32,4096]{2,1,0:T(8,128)(2,1)}, u32[]{:S(2)}) copy-start(bf16[4,32,4096]{2,1,0:T(8,128)(2,1)} %get-tuple-element.698) | copy-start | bytes 3145732 | tf_op jit(solution)/shard_map/while
  197.9 6.9 %copy-start.2 = (f32[1,4096]{1,0:T(1,128)S(1)}, f32[1,4096]{1,0:T(1,128)}, u32[]{:S(2)}) copy-start(f32[1,4096]{1,0:T(1,128)} %get-tuple-element.699) | copy-start | bytes 49156 | tf_op jit(solution)/shard_map/while
  213.8 5.2 copy-start.3
  222.4 7.7 %collective-permute-start = (bf16[32,4096]{1,0:T(8,128)(2,1)S(1)}, bf16[32,4096]{1,0:T(8,128)(2,1)S(1)}, u32[]{:S(2)}, u32[]{:S(2)}) collective-permute-start(bf16[32,4096]{1,0:T(8,128)(2,1)S(1)} %get-tuple-element.638), channel_id=1, source_target_pairs={{32,0},{64,32},{96,64},{128,96},{160,128},{192,160},{224,192},{33,... | collective-permute-start | bytes 786440 | tf_op jit(solution)/shard_map/while/body/eval_jaxpr/ppermute | solution.py:17
  230.1 6.9 %copy-start.1 = (bf16[4,32,4096]{2,1,0:T(8,128)(2,1)S(1)}, bf16[4,32,4096]{2,1,0:T(8,128)(2,1)}, u32[]{:S(2)}) copy-start(bf16[4,32,4096]{2,1,0:T(8,128)(2,1)} %get-tuple-element.698) | copy-start | bytes 3145732 | tf_op jit(solution)/shard_map/while
  230.1 6.9 %copy-start.2 = (f32[1,4096]{1,0:T(1,128)S(1)}, f32[1,4096]{1,0:T(1,128)}, u32[]{:S(2)}) copy-start(f32[1,4096]{1,0:T(1,128)} %get-tuple-element.699) | copy-start | bytes 49156 | tf_op jit(solution)/shard_map/while
  246.0 5.2 copy-start.3
  254.6 7.7 %collective-permute-start = (bf16[32,4096]{1,0:T(8,128)(2,1)S(1)}, bf16[32,4096]{1,0:T(8,128)(2,1)S(1)}, u32[]{:S(2)}, u32[]{:S(2)}) collective-permute-start(bf16[32,4096]{1,0:T(8,128)(2,1)S(1)} %get-tuple-element.638), channel_id=1, source_target_pairs={{32,0},{64,32},{96,64},{128,96},{160,128},{192,160},{224,192},{33,... | collective-permute-start | bytes 786440 | tf_op jit(solution)/shard_map/while/body/eval_jaxpr/ppermute | solution.py:17
  262.3 6.9 %copy-start.1 = (bf16[4,32,4096]{2,1,0:T(8,128)(2,1)S(1)}, bf16[4,32,4096]{2,1,0:T(8,128)(2,1)}, u32[]{:S(2)}) copy-start(bf16[4,32,4096]{2,1,0:T(8,128)(2,1)} %get-tuple-element.698) | copy-start | bytes 3145732 | tf_op jit(solution)/shard_map/while
  262.3 6.9 %copy-start.2 = (f32[1,4096]{1,0:T(1,128)S(1)}, f32[1,4096]{1,0:T(1,128)}, u32[]{:S(2)}) copy-start(f32[1,4096]{1,0:T(1,128)} %get-tuple-element.699) | copy-start | bytes 49156 | tf_op jit(solution)/shard_map/while
  278.2 5.2 copy-start.3
  286.8 7.7 %collective-permute-start = (bf16[32,4096]{1,0:T(8,128)(2,1)S(1)}, bf16[32,4096]{1,0:T(8,128)(2,1)S(1)}, u32[]{:S(2)}, u32[]{:S(2)}) collective-permute-start(bf16[32,4096]{1,0:T(8,128)(2,1)S(1)} %get-tuple-element.638), channel_id=1, source_target_pairs={{32,0},{64,32},{96,64},{128,96},{160,128},{192,160},{224,192},{33,... | collective-permute-start | bytes 786440 | tf_op jit(solution)/shard_map/while/body/eval_jaxpr/ppermute | solution.py:17
  294.5 6.9 %copy-start.1 = (bf16[4,32,4096]{2,1,0:T(8,128)(2,1)S(1)}, bf16[4,32,4096]{2,1,0:T(8,128)(2,1)}, u32[]{:S(2)}) copy-start(bf16[4,32,4096]{2,1,0:T(8,128)(2,1)} %get-tuple-element.698) | copy-start | bytes 3145732 | tf_op jit(solution)/shard_map/while
  294.5 6.9 %copy-start.2 = (f32[1,4096]{1,0:T(1,128)S(1)}, f32[1,4096]{1,0:T(1,128)}, u32[]{:S(2)}) copy-start(f32[1,4096]{1,0:T(1,128)} %get-tuple-element.699) | copy-start | bytes 49156 | tf_op jit(solution)/shard_map/while
  310.4 5.2 copy-start.3
  319.1 7.7 %collective-permute-start = (bf16[32,4096]{1,0:T(8,128)(2,1)S(1)}, bf16[32,4096]{1,0:T(8,128)(2,1)S(1)}, u32[]{:S(2)}, u32[]{:S(2)}) collective-permute-start(bf16[32,4096]{1,0:T(8,128)(2,1)S(1)} %get-tuple-element.638), channel_id=1, source_target_pairs={{32,0},{64,32},{96,64},{128,96},{160,128},{192,160},{224,192},{33,... | collective-permute-start | bytes 786440 | tf_op jit(solution)/shard_map/while/body/eval_jaxpr/ppermute | solution.py:17
  326.7 6.9 %copy-start.1 = (bf16[4,32,4096]{2,1,0:T(8,128)(2,1)S(1)}, bf16[4,32,4096]{2,1,0:T(8,128)(2,1)}, u32[]{:S(2)}) copy-start(bf16[4,32,4096]{2,1,0:T(8,128)(2,1)} %get-tuple-element.698) | copy-start | bytes 3145732 | tf_op jit(solution)/shard_map/while
  326.7 6.9 %copy-start.2 = (f32[1,4096]{1,0:T(1,128)S(1)}, f32[1,4096]{1,0:T(1,128)}, u32[]{:S(2)}) copy-start(f32[1,4096]{1,0:T(1,128)} %get-tuple-element.699) | copy-start | bytes 49156 | tf_op jit(solution)/shard_map/while
  342.6 5.2 copy-start.3
  351.3 7.7 %collective-permute-start = (bf16[32,4096]{1,0:T(8,128)(2,1)S(1)}, bf16[32,4096]{1,0:T(8,128)(2,1)S(1)}, u32[]{:S(2)}, u32[]{:S(2)}) collective-permute-start(bf16[32,4096]{1,0:T(8,128)(2,1)S(1)} %get-tuple-element.638), channel_id=1, source_target_pairs={{32,0},{64,32},{96,64},{128,96},{160,128},{192,160},{224,192},{33,... | collective-permute-start | bytes 786440 | tf_op jit(solution)/shard_map/while/body/eval_jaxpr/ppermute | solution.py:17
  (8 other events, 31.1 us)
Sparse Core Ops, SparseCore 0:
  365.9 234.8 reduce-scatter.1
where the time goes:
time: 614 us; the launch traced here: 609 us
  waiting for transfers between devices  153 us (25%)
  matrix products  148 us (24%)
  blocking collectives  140 us (23%)
  other arithmetic  79.2 us (13%)
  local copies, waits for them, and re-layouts  58.8 us (10%)
  starting transfers between devices  14.1 us (2%)
  between operations  14.1 us (2%)
    psum x1, blocking collectives, shards(): gain_sum = lax.psum(gain_total, 'dp')  140 us
    reduce_scatter x1, waiting for transfers between devices, shards(): lax.psum_scatter(grad_term.astype(jnp.bfloat16), 'dp', scatter_dimension=...  95.1 us
    ppermute x11, waiting for transfers between devices, shifted(): lax.ppermute(value, axis, [(source, source + steps) for source in range(i...  57.6 us
    dot_general x11, matrix products, layer_pieces(): jnp.einsum('rk,dk->rd', key_grad, key_mat, preferred_element_type=jnp.flo...  40.2 us
    dot_general x11, matrix products, layer_pieces(): jnp.dot(normed, key_mat, preferred_element_type=jnp.float32)  34.8 us
    dot_general x11, matrix products, layer_pieces(): jnp.dot(normed, value_mat, preferred_element_type=jnp.float32)  33.7 us
    scatter x11, other arithmetic, advance(): grads_out.at[slot_pick]  30.5 us
    dot_general x11, matrix products, layer_pieces(): jnp.einsum('rk,dk->rd', value_grad, value_mat, preferred_element_type=jnp...  16.2 us
  transfers between devices with their start and end apart: 12, of which 12 were waited for; matrix products, arithmetic and copies ran while one was open for 1% of the time, Pallas kernels for 0%

commit v1 on v0

v1 whole, which is shorter than its diff:
```python
import functools

import jax
import jax.numpy as jnp
from jax import lax
from jax.experimental import pallas as pl
from jax.experimental.pallas import tpu as pltpu
from jax.sharding import PartitionSpec as P

HD = 128
KVH = 4
EPS = 1e-05
NY = 4

f32 = jnp.float32
bf16 = jnp.bfloat16
MESH = pl.DeviceIdType.MESH


def dot(a, b):
    return jnp.dot(a, b, preferred_element_type=f32)


def dot_t(a, b):
    return lax.dot_general(a, b, (((1,), (1,)), ((), ())), preferred_element_type=f32)


def aligned(index, size):
    return pl.ds(pl.multiple_of(index * size, size), size)


def heads(rows, count):
    return jnp.concatenate([rows[:, a * HD : (a + 1) * HD] for a in range(count)], axis=0)


def normalise(x, gain, inv, normed):
    width = x.shape[1]

    def step(r, _):
        rows = aligned(r, 16)
        xb = x[rows, :].astype(f32)
        scale = lax.rsqrt(jnp.sum(xb * xb, axis=1, keepdims=True) * (1.0 / width) + EPS)
        inv[rows, :] = jnp.broadcast_to(scale, (16, 128))
        normed[rows, :] = (xb * scale * gain[...]).astype(bf16)
        return _

    lax.fori_loop(0, x.shape[0] // 16, step, 0)


def project(normed, weights, kv32, kvb):
    for p, w in enumerate(weights):
        cols = slice(p * w.shape[1], (p + 1) * w.shape[1])
        y = dot(normed[...], w[...])
        kv32[:, cols] = y
        kvb[:, cols] = y.astype(bf16)


def probabilities(m, q, kvb, seg, count, probs):
    n_rows, width = q.shape[1], q.shape[2]
    per_group = width // HD // KVH
    n = n_rows * per_group
    rows = aligned(m, n_rows)
    seg_i = jnp.broadcast_to(seg[pl.ds(m, 1), :], (n_rows, n))
    j = lax.broadcasted_iota(jnp.int32, (n_rows, n), 0)
    i = lax.rem(lax.broadcasted_iota(jnp.int32, (n_rows, n), 1), n_rows)
    seg_j = jnp.sum(jnp.where(i == j, seg_i, 0), axis=1, keepdims=True)
    allowed = ((j <= i) & (seg_i * per_group == seg_j) & (j < count)) | (i == j)
    for g in range(KVH):
        keys = kvb[rows, g * HD : (g + 1) * HD]
        queries = heads(q[m, :, g * per_group * HD : (g + 1) * per_group * HD], per_group)
        scores = dot_t(keys, queries) * (HD**-0.5)
        weights = jnp.where(allowed, jnp.exp(scores), 0.0)
        full = weights / jnp.sum(weights, axis=0, keepdims=True)
        probs[m, g] = jnp.where(i < count, full, 0.0)


def attend(m, gin, q, kvb, probs, both):
    n_rows, width = q.shape[1], q.shape[2]
    per_group = width // HD // KVH
    kv_cols = KVH * HD
    rows = aligned(m, n_rows)
    for g in range(KVH):
        values = kvb[rows, kv_cols + g * HD : kv_cols + (g + 1) * HD]
        head_grad = heads(gin[m, g], per_group)
        queries = heads(q[m, :, g * per_group * HD : (g + 1) * per_group * HD], per_group)
        p = probs[m, g]
        prob_grad = dot_t(values, head_grad)
        score_grad = p * (prob_grad - jnp.sum(p * prob_grad, axis=0, keepdims=True)) * (HD**-0.5)
        both[rows, kv_cols + g * HD : kv_cols + (g + 1) * HD] = dot(p.astype(bf16), head_grad).astype(bf16)
        both[rows, g * HD : (g + 1) * HD] = dot(score_grad.astype(bf16), queries).astype(bf16)


def kernel(
    ns, nz, x, q, gain, kw, vw, cot, seg, counts,
    gout, dk, dv, gg,
    inv, normed, normed_t, normed_all, kv32, kvb, probs, kwt, vwt,
    gin, gnext, grads, gacc, gain_y, gain_zs, gain_zr, ring_s, ring_r,
    cot_sem, next_s, next_r, out_sem, nt_s, nt_r, nt_l, kv_s, kv_r, gy_s, gy_r, gz_s, gz_r, ring_ss, ring_rs,
):
    micros, n_rows, width = q.shape
    total = micros * n_rows
    kv_cols = kw.shape[1]
    chunk = width // KVH
    feats = width // (nz * NY)
    sec = lax.axis_index("section")
    dp = lax.axis_index("dp")
    z, y = lax.div(dp, NY), lax.rem(dp, NY)
    is_last = sec == ns - 1
    is_first = sec == 0
    stages = nz.bit_length() - 1
    half = nz // 2

    def along_z(k):
        return lax.rem(z + k + nz, nz)

    def along_y(k):
        return lax.rem(y + k, NY)

    def flipped(b):
        return z + b - 2 * b * lax.rem(lax.div(z, b), 2)

    def device(zz, yy):
        return (sec, zz * NY + yy)

    y_peers = [device(z, along_y(k)) for k in range(1, NY)]
    up, down = device(along_z(1), y), device(along_z(-1), y)
    flips = [device(flipped(1 << i), y) for i in range(stages)]

    def remote(src, dst, ssem, rsem, dev):
        return pltpu.make_async_remote_copy(
            src_ref=src, dst_ref=dst, send_sem=ssem, recv_sem=rsem, device_id=dev, device_id_type=MESH
        )

    barrier = pltpu.get_barrier_semaphore()
    above, below = (lax.rem(sec + 1, ns), dp), (lax.rem(sec + ns - 1, ns), dp)
    greeted = y_peers + [up, down] + flips[1:] + [above, below]
    for peer in greeted:
        pl.semaphore_signal(barrier, inc=1, device_id=peer, device_id_type=MESH)

    def cot_copy(m, g):
        return pltpu.make_async_copy(
            cot.at[m, :, pl.ds(g * chunk, chunk)], gin.at[m, g], cot_sem.at[m, g]
        )

    @pl.when(is_last)
    def _():
        for m in range(micros):
            for g in range(KVH):
                cot_copy(m, g).start()

    normalise(x, gain, inv, normed)
    project(normed, (kw, vw), kv32, kvb)

    def each_probs(m, _):
        probabilities(m, q, kvb, seg, counts[m], probs)
        return _

    lax.fori_loop(0, micros, each_probs, 0)

    def turn(b, _):
        cols = aligned(b, 128)
        kwt[:, cols] = kw[cols, :].T
        vwt[:, cols] = vw[cols, :].T
        first = b * 128
        owner = lax.div(first, feats)
        at = lax.div(owner, NY) * feats + lax.rem(first, feats)
        normed_t[lax.rem(owner, NY), pl.ds(pl.multiple_of(at, 128), 128), :] = normed[:, cols].T
        return _

    lax.fori_loop(0, width // 128, turn, 0)
    gacc[...] = jnp.zeros_like(gacc)

    pl.semaphore_wait(barrier, len(greeted))

    def nt_copy(k):
        return remote(
            normed_t.at[along_y(k)], normed_all.at[:, pl.ds(k * total, total)], nt_s.at[k], nt_r.at[k], y_peers[k - 1]
        )

    for k in range(1, NY):
        nt_copy(k).start()
    own_nt = pltpu.make_async_copy(normed_t.at[y], normed_all.at[:, pl.ds(0, total)], nt_l)
    own_nt.start()

    def next_copy(m, g):
        return remote(gnext.at[m, g], gin.at[m, g], next_s.at[m, g], next_r.at[m, g], below)

    def out_copy(m, g):
        return pltpu.make_async_copy(
            gnext.at[m, g], gout.at[m, :, pl.ds(g * chunk, chunk)], out_sem.at[m, g]
        )

    def kv_copy(m, k):
        rows = aligned(m, n_rows)
        to = pl.ds(pl.multiple_of(k * total + m * n_rows, n_rows), n_rows)
        return remote(grads.at[rows, :], grads.at[to, :], kv_s.at[k, m], kv_r.at[k, m], y_peers[k - 1])

    def layer(m, carry):
        @pl.when(is_last)
        def _():
            for g in range(KVH):
                cot_copy(m, g).wait()

        @pl.when(jnp.logical_not(is_last))
        def _():
            for g in range(KVH):
                next_copy(m, g).wait_recv()

        attend(m, gin, q, kvb, probs, grads)
        rows = aligned(m, n_rows)
        both = grads[rows, :]
        scale = inv[rows, 0:1]
        pulled = jnp.sum(both.astype(f32) * kv32[rows, :], axis=1, keepdims=True) * (
            scale * scale * (1.0 / width)
        )
        for g in range(KVH):
            cols = slice(g * chunk, (g + 1) * chunk)
            grad = (dot(both[:, :kv_cols], kwt[:, cols]) + dot(both[:, kv_cols:], vwt[:, cols])) * scale
            xb = x[rows, cols].astype(f32)
            gnext[m, g] = (gin[m, g].astype(f32) + grad * gain[:, cols] - xb * pulled).astype(bf16)

            @pl.when(jnp.logical_not(is_first))
            def _():
                next_copy(m, g).start()

            out_copy(m, g).start()
            term = grad * xb
            gacc[:, cols] += term[0:8] + term[8:16] + term[16:24] + term[24:32]
        for k in range(1, NY):
            kv_copy(m, k).start()
        return carry

    lax.fori_loop(0, micros, layer, 0)

    part = width // 8
    gsum = jnp.sum(gacc[...], axis=0, keepdims=True)
    for r in range(8):
        gain_y[0, r : r + 1, :] = gsum[:, r * part : (r + 1) * part]

    def gy_copy(k):
        return remote(gain_y.at[0], gain_y.at[k], gy_s.at[k], gy_r.at[k], y_peers[k - 1])

    def gz_copy(i):
        return remote(gain_zs.at[i], gain_zr.at[i], gz_s.at[i], gz_r.at[i], flips[i])

    for k in range(1, NY):
        gy_copy(k).start()

    def gain_stage(i):
        if i == 0:
            for k in range(1, NY):
                gy_copy(k).wait_recv()
            summed = gain_y[0]
            for k in range(1, NY):
                summed = summed + gain_y[k]
        else:
            gz_copy(i - 1).wait_recv()
            summed = gain_zs[i - 1] + gain_zr[i - 1]
        if i < stages:
            gain_zs[i] = summed
            gz_copy(i).start()
        else:
            for r in range(8):
                gg[:, r * part : (r + 1) * part] = summed[r : r + 1, :]

    own_nt.wait()
    for k in range(1, NY):
        nt_copy(k).wait_recv()

    def kv_waits(m, _):
        for k in range(1, NY):
            kv_copy(m, k).wait_recv()
        return _

    lax.fori_loop(0, micros, kv_waits, 0)

    def piece(zz, h):
        return dot(normed_all[aligned(zz, feats), :], grads[:, h * kv_cols : (h + 1) * kv_cols])

    def ring_copy(way, t, h):
        return remote(
            ring_s.at[way, t, h], ring_r.at[way, t, h], ring_ss.at[way, t, h], ring_rs.at[way, t, h],
            (down, up)[way],
        )

    for t in range(half):
        sums = {}
        for way in range(2):
            target = along_z((t - half) if way == 0 else (half - t))
            for h in range(2):
                if t > 0 or h == way:
                    sums[way, h] = piece(target, h)
        for h in range(2):
            for way in range(2):
                if (way, h) in sums:
                    value = sums[way, h]
                    if t > 1 or (t == 1 and h == way):
                        ring_copy(way, t - 1, h).wait_recv()
                        value = value + ring_r[way, t - 1, h].astype(f32)
                    ring_s[way, t, h] = value.astype(bf16)
                    ring_copy(way, t, h).start()
        if t <= stages:
            gain_stage(t)
    for t in range(half, stages + 1):
        gain_stage(t)
    own = [piece(z, h) for h in range(2)]
    for h, out in enumerate((dk, dv)):
        value = own[h]
        for way in range(2):
            ring_copy(way, half - 1, h).wait_recv()
            value = value + ring_r[way, half - 1, h].astype(f32)
        out[...] = value

    def sent(m, carry):
        for g in range(KVH):
            @pl.when(jnp.logical_not(is_first))
            def _():
                next_copy(m, g).wait_send()

            out_copy(m, g).wait()
        for k in range(1, NY):
            kv_copy(m, k).wait_send()
        return carry

    lax.fori_loop(0, micros, sent, 0)
    for k in range(1, NY):
        nt_copy(k).wait_send()
        gy_copy(k).wait_send()
    for i in range(stages):
        gz_copy(i).wait_send()
    for t in range(half):
        for way in range(2):
            for h in range(2):
                if t > 0 or h == way:
                    ring_copy(way, t, h).wait_send()


def shards(ns, nd, saved_inputs, saved_queries, norm_gain, key_weight, value_weight, out_cotangent, token_counts, segment_ids):
    micros, n_rows, width = saved_inputs.shape[2:]
    kv_cols = key_weight.shape[2]
    total = micros * n_rows
    nz = nd // NY
    per_group = width // HD // KVH
    chunk = width // KVH
    feats = width // nd
    half = nz // 2
    stages = nz.bit_length() - 1
    vmem = pl.BlockSpec(memory_space=pltpu.VMEM)
    anywhere = pl.BlockSpec(memory_space=pl.ANY)
    dma = pltpu.SemaphoreType.DMA
    segments = jnp.tile(segment_ids[0], (1, per_group))
    gout, dk, dv, gg = pl.pallas_call(
        functools.partial(kernel, ns, nz),
        out_shape=(
            jax.ShapeDtypeStruct((micros, n_rows, width), bf16),
            jax.ShapeDtypeStruct((feats, kv_cols), f32),
            jax.ShapeDtypeStruct((feats, kv_cols), f32),
            jax.ShapeDtypeStruct((1, width), f32),
        ),
        in_specs=[vmem, vmem, vmem, vmem, vmem, anywhere, vmem, pl.BlockSpec(memory_space=pltpu.SMEM)],
        out_specs=(anywhere, vmem, vmem, vmem),
        scratch_shapes=[
            pltpu.VMEM((total, 128), f32),
            pltpu.VMEM((total, width), bf16),
            pltpu.VMEM((NY, nz * feats, total), bf16),
            pltpu.VMEM((nz * feats, NY * total), bf16),
            pltpu.VMEM((total, 2 * kv_cols), f32),
            pltpu.VMEM((total, 2 * kv_cols), bf16),
            pltpu.VMEM((micros, KVH, n_rows, n_rows * per_group), f32),
            pltpu.VMEM((kv_cols, width), bf16),
            pltpu.VMEM((kv_cols, width), bf16),
            pltpu.VMEM((micros, KVH, n_rows, chunk), bf16),
            pltpu.VMEM((micros, KVH, n_rows, chunk), bf16),
            pltpu.VMEM((NY * total, 2 * kv_cols), bf16),
            pltpu.VMEM((8, width), f32),
            pltpu.VMEM((NY, 8, width // 8), f32),
            pltpu.VMEM((stages, 8, width // 8), f32),
            pltpu.VMEM((stages, 8, width // 8), f32),
            pltpu.VMEM((2, half, 2, feats, kv_cols), bf16),
            pltpu.VMEM((2, half, 2, feats, kv_cols), bf16),
            dma((micros, KVH)),
            dma((micros, KVH)),
            dma((micros, KVH)),
            dma((micros, KVH)),
            dma((NY,)),
            dma((NY,)),
            dma,
            dma((NY, micros)),
            dma((NY, micros)),
            dma((NY,)),
            dma((NY,)),
            dma((stages,)),
            dma((stages,)),
            dma((2, half, 2)),
            dma((2, half, 2)),
        ],
        compiler_params=pltpu.CompilerParams(
            collective_id=0, has_side_effects=True, vmem_limit_bytes=48 * 2**20
        ),
        name="layers_backward",
    )(
        saved_inputs[0, 0].reshape(total, width),
        saved_queries[0, 0],
        norm_gain,
        key_weight[0],
        value_weight[0],
        out_cotangent[0],
        segments,
        token_counts[0],
    )
    return gout[None, None], dk[None], dv[None], gg


def solution(mesh):
    placed = (
        P("section", "dp", None, None, None),
        P("section", "dp", None, None, None),
        P("section", None),
        P("section", None, None),
        P("section", None, None),
        P("dp", None, None, None),
        P("dp", None),
        P("dp", None, None),
    )
    return jax.shard_map(
        functools.partial(shards, mesh.shape["section"], mesh.shape["dp"]),
        mesh=mesh,
        in_specs=placed,
        out_specs=(
            P("section", "dp", None, None, None),
            P("section", "dp", None),
            P("section", "dp", None),
            P("section", None),
        ),
        check_vma=False,
    )
```

time: 614 us -> 99.8 us (0.16)
  waiting for transfers between devices: 153 us -> 0 us
  matrix products: 148 us -> 0 us
  blocking collectives: 140 us -> 0 us
  Pallas kernels: 0 us -> 90.1 us
  other arithmetic: 79.2 us -> 0 us
  local copies, waits for them, and re-layouts: 58.8 us -> 8.79 us
  starting transfers between devices: 14.1 us -> 0 us
  between operations: 14.1 us -> 0.65 us
    dot_general x89 -> x0, matrix products: 148 us -> none  [the longest x11 40.2 us: layer_pieces(): jnp.einsum('rk,dk->rd', key_grad, key_mat, preferred_element_type=jnp.flo...]
    psum x1 -> x0, blocking collectives: 140 us -> none  [shards(): gain_sum = lax.psum(gain_total, 'dp')]
    reduce_scatter x1 -> x0, waiting for transfers between devices: 95.1 us -> none  [shards(): lax.psum_scatter(grad_term.astype(jnp.bfloat16), 'dp', scatter_dimension=...]
    pallas_call x0 -> x1, Pallas kernels: none -> 90.1 us  [shards(): pl.pallas_call(functools.partial(kernel, ns, nz), out_shape=(jax.ShapeDty...]
    ppermute x11 -> x0, waiting for transfers between devices: 57.6 us -> none  [shifted(): lax.ppermute(value, axis, [(source, source + steps) for source in range(i...]
    scatter x22 -> x0, other arithmetic: 36.9 us -> none  [the longest x11 30.5 us: advance(): grads_out.at[slot_pick]]
    dynamic_slice x22 -> x0, local copies, waits for them, and re-layouts: 25.2 us -> none  [the longest x11 14.5 us: advance(): counts[slot_pick]]
    ppermute x11 -> x0, starting transfers between devices: 14.1 us -> none  [shifted(): lax.ppermute(value, axis, [(source, source + steps) for source in range(i...]
  transfers between devices with their start and end apart: 12 -> 0, of which waited for: 12 -> 0; matrix products, arithmetic and copies ran while one was open for 1% -> 0% of each run, Pallas kernels for 0% -> 0%
where the time goes in v1:
time: 99.8 us; the launch traced here: 99.6 us
  Pallas kernels  90.1 us (90%)
  local copies, waits for them, and re-layouts  8.79 us (9%)
    pallas_call x1, Pallas kernels, shards(): pl.pallas_call(functools.partial(kernel, ns, nz), out_shape=(jax.ShapeDty...  90.1 us
    unnamed x14, local copies, waits for them, and re-layouts  8.03 us

profile of v1, /device:TPU:32, one launch (start us, length us, event | category | flops | bytes accessed | tf_op | source)
XLA Modules:
  0.0 99.6 jit_solution(15631011843068550534)
XLA Ops:
  0.6 0.7 tile.11
  1.3 0.1 tile.12.seg
  1.4 0.0 copy-start
  1.4 1.2 %copy-done = bf16[1,1,4,32,4096]{4,3,2,1,0:T(8,128)(2,1)S(1)} copy-done((bf16[1,1,4,32,4096]{4,3,2,1,0:T(8,128)(2,1)S(1)}, bf16[1,1,4,32,4096]{4,3,2,1,0:T(8,128)(2,1)}, u32[]{:S(2)}) %copy-start) | copy-done | bytes 1048600
  2.6 0.0 copy-start.1
  2.6 1.2 %copy-done.1 = bf16[1,1,4,32,4096]{4,3,2,1,0:T(8,128)(2,1)S(1)} copy-done((bf16[1,1,4,32,4096]{4,3,2,1,0:T(8,128)(2,1)S(1)}, bf16[1,1,4,32,4096]{4,3,2,1,0:T(8,128)(2,1)}, u32[]{:S(2)}) %copy-start.1) | copy-done | bytes 1048600
  3.8 0.0 copy-start.2
  3.8 1.2 %copy-done.2 = bf16[1,4,32,4096]{3,2,1,0:T(8,128)(2,1)S(1)} copy-done((bf16[1,4,32,4096]{3,2,1,0:T(8,128)(2,1)S(1)}, bf16[1,4,32,4096]{3,2,1,0:T(8,128)(2,1)}, u32[]{:S(2)}) %copy-start.2) | copy-done | bytes 1048600
  5.1 0.0 copy-start.3
  5.1 0.7 copy-done.3
  5.8 0.0 copy-start.4
  5.8 0.7 copy-done.4
  6.4 90.1 %layers_backward.1 = (bf16[4,32,4096]{2,1,0:T(8,128)(2,1)S(1)}, f32[128,512]{1,0:T(8,128)S(1)}, f32[128,512]{1,0:T(8,128)S(1)}, f32[1,4096]{1,0:T(1,128)S(1)}) custom-call(bf16[128,4096]{1,0:T(8,128)(2,1)S(1)} %bitcast.11, bf16[4,32,4096]{2,1,0:T(8,128)(2,1)S(1)} %bitcast.12, f32[1,4096]{1,0:T(1,128)S(1)} %copy-done.3, bf16[4096,512]{1,0:T(8,128)(2,1)} %bitcast.17, ...), custom_call_target="tpu_custom_call" | custom-call | tf_op jit(solution)/shard_map/layers_backward/pallas_call | solution.py:352
  96.6 1.0 copy.16
  97.6 0.7 copy.17
  98.3 0.7 copy.18
  99.0 0.6 copy.19
Async XLA Ops:
  1.4 1.2 %copy-start = (bf16[1,1,4,32,4096]{4,3,2,1,0:T(8,128)(2,1)S(1)}, bf16[1,1,4,32,4096]{4,3,2,1,0:T(8,128)(2,1)}, u32[]{:S(2)}) copy-start(bf16[1,1,4,32,4096]{4,3,2,1,0:T(8,128)(2,1)} %param.8) | copy-start | bytes 3145732
  2.6 1.2 %copy-start.1 = (bf16[1,1,4,32,4096]{4,3,2,1,0:T(8,128)(2,1)S(1)}, bf16[1,1,4,32,4096]{4,3,2,1,0:T(8,128)(2,1)}, u32[]{:S(2)}) copy-start(bf16[1,1,4,32,4096]{4,3,2,1,0:T(8,128)(2,1)} %param.9) | copy-start | bytes 3145732
  3.8 1.2 %copy-start.2 = (bf16[1,4,32,4096]{3,2,1,0:T(8,128)(2,1)S(1)}, bf16[1,4,32,4096]{3,2,1,0:T(8,128)(2,1)}, u32[]{:S(2)}) copy-start(bf16[1,4,32,4096]{3,2,1,0:T(8,128)(2,1)} %param.13) | copy-start | bytes 3145732
  5.1 0.7 copy-start.3
  5.8 0.7 copy-start.4

commit v2 on v1

--- a/solution.py
+++ b/solution.py
@@ -11,6 +11,7 @@
 KVH = 4
 EPS = 1e-05
 NY = 4
+PARTS = 4
 
 f32 = jnp.float32
 bf16 = jnp.bfloat16
@@ -47,20 +48,26 @@
     lax.fori_loop(0, x.shape[0] // 16, step, 0)
 
 
-def project(normed, weights, kv32, kvb):
-    for p, w in enumerate(weights):
+def project(c, parts, normed, weights, turned, kv32):
+    depth = normed.shape[1] // parts
+    rows = aligned(c, depth)
+    features = normed[:, rows]
+    for p, (w, wt) in enumerate(zip(weights, turned)):
         cols = slice(p * w.shape[1], (p + 1) * w.shape[1])
-        y = dot(normed[...], w[...])
-        kv32[:, cols] = y
-        kvb[:, cols] = y.astype(bf16)
-
-
-def probabilities(m, q, kvb, seg, count, probs):
+        block = w[rows, :]
+        kv32[:, cols] += dot(features, block)
+        wt[:, rows] = block.T
+
+
+def probabilities(m, q, kvb, seg, counts, probs):
     n_rows, width = q.shape[1], q.shape[2]
     per_group = width // HD // KVH
     n = n_rows * per_group
     rows = aligned(m, n_rows)
-    seg_i = jnp.broadcast_to(seg[pl.ds(m, 1), :], (n_rows, n))
+    seg_row = seg[pl.ds(m, 1), :]
+    seg_i = jnp.broadcast_to(jnp.concatenate([seg_row] * per_group, axis=1), (n_rows, n))
+    micro = lax.broadcasted_iota(jnp.int32, counts.shape, 1)
+    count = jnp.sum(jnp.where(micro == m, counts[...], 0), axis=1, keepdims=True)
     j = lax.broadcasted_iota(jnp.int32, (n_rows, n), 0)
     i = lax.rem(lax.broadcasted_iota(jnp.int32, (n_rows, n), 1), n_rows)
     seg_j = jnp.sum(jnp.where(i == j, seg_i, 0), axis=1, keepdims=True)
@@ -74,30 +81,30 @@
         probs[m, g] = jnp.where(i < count, full, 0.0)
 
 
-def attend(m, gin, q, kvb, probs, both):
+def attend(m, g, incoming, q, kvb, probs, both):
     n_rows, width = q.shape[1], q.shape[2]
     per_group = width // HD // KVH
     kv_cols = KVH * HD
     rows = aligned(m, n_rows)
-    for g in range(KVH):
-        values = kvb[rows, kv_cols + g * HD : kv_cols + (g + 1) * HD]
-        head_grad = heads(gin[m, g], per_group)
-        queries = heads(q[m, :, g * per_group * HD : (g + 1) * per_group * HD], per_group)
-        p = probs[m, g]
-        prob_grad = dot_t(values, head_grad)
-        score_grad = p * (prob_grad - jnp.sum(p * prob_grad, axis=0, keepdims=True)) * (HD**-0.5)
-        both[rows, kv_cols + g * HD : kv_cols + (g + 1) * HD] = dot(p.astype(bf16), head_grad).astype(bf16)
-        both[rows, g * HD : (g + 1) * HD] = dot(score_grad.astype(bf16), queries).astype(bf16)
+    values = kvb[rows, kv_cols + g * HD : kv_cols + (g + 1) * HD]
+    head_grad = heads(incoming, per_group)
+    queries = heads(q[m, :, g * per_group * HD : (g + 1) * per_group * HD], per_group)
+    p = probs[m, g]
+    prob_grad = dot_t(values, head_grad)
+    score_grad = p * (prob_grad - jnp.sum(p * prob_grad, axis=0, keepdims=True)) * (HD**-0.5)
+    both[rows, kv_cols + g * HD : kv_cols + (g + 1) * HD] = dot(p.astype(bf16), head_grad).astype(bf16)
+    both[rows, g * HD : (g + 1) * HD] = dot(score_grad.astype(bf16), queries).astype(bf16)
 
 
 def kernel(
-    ns, nz, x, q, gain, kw, vw, cot, seg, counts,
+    ns, nz, x_in, q_in, gain_in, kw_in, vw_in, cot, seg_in, counts_in,
     gout, dk, dv, gg,
-    inv, normed, normed_t, normed_all, kv32, kvb, probs, kwt, vwt,
+    x, q, gain, kw, vw, seg, counts, inv, normed, normed_t, normed_all, kv32, kvb, probs, kwt, vwt,
     gin, gnext, grads, gacc, gain_y, gain_zs, gain_zr, ring_s, ring_r,
-    cot_sem, next_s, next_r, out_sem, nt_s, nt_r, nt_l, kv_s, kv_r, gy_s, gy_r, gz_s, gz_r, ring_ss, ring_rs,
+    x_sem, q_sem, gain_sem, seg_sem, counts_sem, w_sem, cot_sem, next_s, next_r, out_sem, nt_s, nt_r, nt_l, kv_s, kv_r, gy_s, gy_r, gz_s, gz_r, ring_ss, ring_rs,
 ):
     micros, n_rows, width = q.shape
+    parts = w_sem.shape[1]
     total = micros * n_rows
     kv_cols = kw.shape[1]
     chunk = width // KVH
@@ -106,7 +113,6 @@
     dp = lax.axis_index("dp")
     z, y = lax.div(dp, NY), lax.rem(dp, NY)
     is_last = sec == ns - 1
-    is_first = sec == 0
     stages = nz.bit_length() - 1
     half = nz // 2
 
@@ -130,6 +136,25 @@
         return pltpu.make_async_remote_copy(
             src_ref=src, dst_ref=dst, send_sem=ssem, recv_sem=rsem, device_id=dev, device_id_type=MESH
         )
+
+    def w_copy(p, c):
+        rows = aligned(c, width // parts)
+        return pltpu.make_async_copy((kw_in, vw_in)[p].at[rows, :], (kw, vw)[p].at[rows, :], w_sem.at[p, c])
+
+    x_copy = pltpu.make_async_copy(x_in, x, x_sem)
+    q_copy = pltpu.make_async_copy(q_in, q, q_sem)
+    gain_copy = pltpu.make_async_copy(gain_in, gain, gain_sem)
+    seg_copy = pltpu.make_async_copy(seg_in, seg, seg_sem)
+    counts_copy = pltpu.make_async_copy(counts_in, counts, counts_sem)
+    x_copy.start()
+    gain_copy.start()
+    for c in range(parts):
+        for p in range(2):
+            w_copy(p, c).start()
+        if c == 0:
+            q_copy.start()
+            seg_copy.start()
+            counts_copy.start()
 
     barrier = pltpu.get_barrier_semaphore()
     above, below = (lax.rem(sec + 1, ns), dp), (lax.rem(sec + ns - 1, ns), dp)
@@ -139,7 +164,7 @@
 
     def cot_copy(m, g):
         return pltpu.make_async_copy(
-            cot.at[m, :, pl.ds(g * chunk, chunk)], gin.at[m, g], cot_sem.at[m, g]
+            cot.at[m, :, pl.ds(g * chunk, chunk)], gin.at[1, m, g], cot_sem.at[m, g]
         )
 
     @pl.when(is_last)
@@ -148,27 +173,34 @@
             for g in range(KVH):
                 cot_copy(m, g).start()
 
+    kv32[...] = jnp.zeros_like(kv32)
+    gacc[...] = jnp.zeros_like(gacc)
+    x_copy.wait()
+    gain_copy.wait()
     normalise(x, gain, inv, normed)
-    project(normed, (kw, vw), kv32, kvb)
-
-    def each_probs(m, _):
-        probabilities(m, q, kvb, seg, counts[m], probs)
-        return _
-
-    lax.fori_loop(0, micros, each_probs, 0)
-
-    def turn(b, _):
-        cols = aligned(b, 128)
-        kwt[:, cols] = kw[cols, :].T
-        vwt[:, cols] = vw[cols, :].T
+
+    def each_part(c, carry):
+        for p in range(2):
+            w_copy(p, c).wait()
+        project(c, parts, normed, (kw, vw), (kwt, vwt), kv32)
+        return carry
+
+    lax.fori_loop(0, parts, each_part, 0)
+    kvb[...] = kv32[...].astype(bf16)
+    q_copy.wait()
+    seg_copy.wait()
+    counts_copy.wait()
+
+    def each_probs(m, carry):
+        probabilities(m, q, kvb, seg, counts, probs)
+        return carry
+
+    def turn(b, carry):
         first = b * 128
         owner = lax.div(first, feats)
         at = lax.div(owner, NY) * feats + lax.rem(first, feats)
-        normed_t[lax.rem(owner, NY), pl.ds(pl.multiple_of(at, 128), 128), :] = normed[:, cols].T
-        return _
-
-    lax.fori_loop(0, width // 128, turn, 0)
-    gacc[...] = jnp.zeros_like(gacc)
+        normed_t[lax.rem(owner, NY), pl.ds(pl.multiple_of(at, 128), 128), :] = normed[:, aligned(b, 128)].T
+        return carry
 
     pl.semaphore_wait(barrier, len(greeted))
 
@@ -177,13 +209,16 @@
             normed_t.at[along_y(k)], normed_all.at[:, pl.ds(k * total, total)], nt_s.at[k], nt_r.at[k], y_peers[k - 1]
         )
 
-    for k in range(1, NY):
-        nt_copy(k).start()
     own_nt = pltpu.make_async_copy(normed_t.at[y], normed_all.at[:, pl.ds(0, total)], nt_l)
-    own_nt.start()
+
+    def exchange_normed():
+        lax.fori_loop(0, width // 128, turn, 0)
+        for k in range(1, NY):
+            nt_copy(k).start()
+        own_nt.start()
 
     def next_copy(m, g):
-        return remote(gnext.at[m, g], gin.at[m, g], next_s.at[m, g], next_r.at[m, g], below)
+        return remote(gnext.at[m, g], gin.at[0, m, g], next_s.at[m, g], next_r.at[m, g], below)
 
     def out_copy(m, g):
         return pltpu.make_async_copy(
@@ -195,18 +230,18 @@
         to = pl.ds(pl.multiple_of(k * total + m * n_rows, n_rows), n_rows)
         return remote(grads.at[rows, :], grads.at[to, :], kv_s.at[k, m], kv_r.at[k, m], y_peers[k - 1])
 
-    def layer(m, carry):
-        @pl.when(is_last)
-        def _():
-            for g in range(KVH):
+    def layer(last, m, carry):
+        incoming = gin.at[int(last)]
+        if last:
+            probabilities(m, q, kvb, seg, counts, probs)
+        for g in range(KVH):
+            if last:
                 cot_copy(m, g).wait()
-
-        @pl.when(jnp.logical_not(is_last))
-        def _():
-            for g in range(KVH):
+            else:
                 next_copy(m, g).wait_recv()
-
-        attend(m, gin, q, kvb, probs, grads)
+            attend(m, g, incoming[m, g], q, kvb, probs, grads)
+        for k in range(1, NY):
+            kv_copy(m, k).start()
         rows = aligned(m, n_rows)
         both = grads[rows, :]
         scale = inv[rows, 0:1]
@@ -217,20 +252,24 @@
             cols = slice(g * chunk, (g + 1) * chunk)
             grad = (dot(both[:, :kv_cols], kwt[:, cols]) + dot(both[:, kv_cols:], vwt[:, cols])) * scale
             xb = x[rows, cols].astype(f32)
-            gnext[m, g] = (gin[m, g].astype(f32) + grad * gain[:, cols] - xb * pulled).astype(bf16)
-
-            @pl.when(jnp.logical_not(is_first))
-            def _():
-                next_copy(m, g).start()
-
-            out_copy(m, g).start()
+            gnext[m, g] = (incoming[m, g].astype(f32) + grad * gain[:, cols] - xb * pulled).astype(bf16)
+            next_copy(m, g).start()
             term = grad * xb
             gacc[:, cols] += term[0:8] + term[8:16] + term[16:24] + term[24:32]
-        for k in range(1, NY):
-            kv_copy(m, k).start()
+        for g in range(KVH):
+            out_copy(m, g).start()
         return carry
 
-    lax.fori_loop(0, micros, layer, 0)
+    @pl.when(is_last)
+    def _():
+        lax.fori_loop(0, micros, functools.partial(layer, True), 0)
+        exchange_normed()
+
+    @pl.when(jnp.logical_not(is_last))
+    def _():
+        lax.fori_loop(0, micros, each_probs, 0)
+        exchange_normed()
+        lax.fori_loop(0, micros, functools.partial(layer, False), 0)
 
     part = width // 8
     gsum = jnp.sum(gacc[...], axis=0, keepdims=True)
@@ -313,10 +352,7 @@
 
     def sent(m, carry):
         for g in range(KVH):
-            @pl.when(jnp.logical_not(is_first))
-            def _():
-                next_copy(m, g).wait_send()
-
+            next_copy(m, g).wait_send()
             out_copy(m, g).wait()
         for k in range(1, NY):
             kv_copy(m, k).wait_send()
@@ -326,6 +362,13 @@
     for k in range(1, NY):
         nt_copy(k).wait_send()
         gy_copy(k).wait_send()
+
+    @pl.when(is_last)
+    def _():
+        for m in range(micros):
+            for g in range(KVH):
+                next_copy(m, g).wait_recv()
+
     for i in range(stages):
         gz_copy(i).wait_send()
     for t in range(half):
@@ -333,6 +376,15 @@
             for h in range(2):
                 if t > 0 or h == way:
                     ring_copy(way, t, h).wait_send()
+
+
+def store(*refs):
+    count = len(refs) // 2
+    copies = [pltpu.make_async_copy(refs[r], refs[count + r], refs[-1].at[r]) for r in range(count)]
+    for copy in copies:
+        copy.start()
+    for copy in copies:
+        copy.wait()
 
 
 def shards(ns, nd, saved_inputs, saved_queries, norm_gain, key_weight, value_weight, out_cotangent, token_counts, segment_ids):
@@ -346,9 +398,8 @@
     half = nz // 2
     stages = nz.bit_length() - 1
     vmem = pl.BlockSpec(memory_space=pltpu.VMEM)
-    anywhere = pl.BlockSpec(memory_space=pl.ANY)
+    hbm = pl.BlockSpec(memory_space=pltpu.HBM)
     dma = pltpu.SemaphoreType.DMA
-    segments = jnp.tile(segment_ids[0], (1, per_group))
     gout, dk, dv, gg = pl.pallas_call(
         functools.partial(kernel, ns, nz),
         out_shape=(
@@ -357,9 +408,16 @@
             jax.ShapeDtypeStruct((feats, kv_cols), f32),
             jax.ShapeDtypeStruct((1, width), f32),
         ),
-        in_specs=[vmem, vmem, vmem, vmem, vmem, anywhere, vmem, pl.BlockSpec(memory_space=pltpu.SMEM)],
-        out_specs=(anywhere, vmem, vmem, vmem),
+        in_specs=[hbm] * 8,
+        out_specs=(hbm, vmem, vmem, vmem),
         scratch_shapes=[
+            pltpu.VMEM((total, width), bf16),
+            pltpu.VMEM((micros, n_rows, width), bf16),
+            pltpu.VMEM((1, width), f32),
+            pltpu.VMEM((width, kv_cols), bf16),
+            pltpu.VMEM((width, kv_cols), bf16),
+            pltpu.VMEM((micros, n_rows), jnp.int32),
+            pltpu.VMEM((1, micros), jnp.int32),
             pltpu.VMEM((total, 128), f32),
             pltpu.VMEM((total, width), bf16),
             pltpu.VMEM((NY, nz * feats, total), bf16),
@@ -369,7 +427,7 @@
             pltpu.VMEM((micros, KVH, n_rows, n_rows * per_group), f32),
             pltpu.VMEM((kv_cols, width), bf16),
             pltpu.VMEM((kv_cols, width), bf16),
-            pltpu.VMEM((micros, KVH, n_rows, chunk), bf16),
+            pltpu.VMEM((2, micros, KVH, n_rows, chunk), bf16),
             pltpu.VMEM((micros, KVH, n_rows, chunk), bf16),
             pltpu.VMEM((NY * total, 2 * kv_cols), bf16),
             pltpu.VMEM((8, width), f32),
@@ -378,6 +436,12 @@
             pltpu.VMEM((stages, 8, width // 8), f32),
             pltpu.VMEM((2, half, 2, feats, kv_cols), bf16),
             pltpu.VMEM((2, half, 2, feats, kv_cols), bf16),
+            dma,
+            dma,
+            dma,
+            dma,
+            dma,
+            dma((2, PARTS)),
             dma((micros, KVH)),
             dma((micros, KVH)),
             dma((micros, KVH)),
@@ -395,7 +459,7 @@
             dma((2, half, 2)),
         ],
         compiler_params=pltpu.CompilerParams(
-            collective_id=0, has_side_effects=True, vmem_limit_bytes=48 * 2**20
+            collective_id=0, has_side_effects=True, vmem_limit_bytes=60 * 2**20
         ),
         name="layers_backward",
     )(
@@ -405,9 +469,19 @@
         key_weight[0],
         value_weight[0],
         out_cotangent[0],
-        segments,
-        token_counts[0],
+        segment_ids[0],
+        token_counts,
     )
+    results = (gout, dk, dv, gg)
+    gout, dk, dv, gg = pl.pallas_call(
+        store,
+        out_shape=tuple(jax.ShapeDtypeStruct(r.shape, r.dtype) for r in results),
+        in_specs=[vmem] * len(results),
+        out_specs=(hbm,) * len(results),
+        scratch_shapes=[dma((len(results),))],
+        compiler_params=pltpu.CompilerParams(vmem_limit_bytes=60 * 2**20),
+        name="store_results",
+    )(*results)
     return gout[None, None], dk[None], dv[None], gg
 
 

time: 99.8 us -> 90.1 us (0.903)
  local copies, waits for them, and re-layouts: 8.79 us -> 0 us
    unnamed x14 -> x0, local copies, waits for them, and re-layouts: 8.03 us -> none
    pallas_call x1, Pallas kernels: 90.1 us -> 86.8 us  [shards(): pl.pallas_call(functools.partial(kernel, ns, nz), out_shape=(jax.ShapeDty...]
    pallas_call x0 -> x1, Pallas kernels: none -> 2.52 us  [shards(): pl.pallas_call(store, out_shape=tuple((jax.ShapeDtypeStruct(r.shape, r.dt...]
where the time goes in v2:
time: 90.1 us; the launch traced here: 90 us
  Pallas kernels  89.3 us (99%)
    pallas_call x1, Pallas kernels, shards(): pl.pallas_call(functools.partial(kernel, ns, nz), out_shape=(jax.ShapeDty...  86.8 us
    pallas_call x1, Pallas kernels, shards(): pl.pallas_call(store, out_shape=tuple((jax.ShapeDtypeStruct(r.shape, r.dt...  2.52 us

profile of v2, /device:TPU:32, one launch (start us, length us, event | category | flops | bytes accessed | tf_op | source)
XLA Modules:
  0.0 90.0 jit_solution(12206095411936289841)
XLA Ops:
  0.6 86.8 %layers_backward.1 = (bf16[4,32,4096]{2,1,0:T(8,128)(2,1)}, f32[128,512]{1,0:T(8,128)}, f32[128,512]{1,0:T(8,128)}, f32[1,4096]{1,0:T(1,128)}) custom-call(bf16[128,4096]{1,0:T(8,128)(2,1)} %bitcast.11, bf16[4,32,4096]{2,1,0:T(8,128)(2,1)} %bitcast.12, f32[1,4096]{1,0:T(1,128)} %gain_in.1, bf16[4096,512]{1,0:T(8,128)(2,1)} %bitcast.9, ...), custom_call_target="tpu_custom_call" | custom-call | tf_op jit(solution)/shard_map/layers_backward/pallas_call | solution.py:403
  87.4 2.5 %store_results.1 = (bf16[4,32,4096]{2,1,0:T(8,128)(2,1)}, f32[128,512]{1,0:T(8,128)}, f32[128,512]{1,0:T(8,128)}, f32[1,4096]{1,0:T(1,128)}) custom-call(bf16[4,32,4096]{2,1,0:T(8,128)(2,1)} %get-tuple-element.12.refs_0_, f32[128,512]{1,0:T(8,128)} %get-tuple-element.13.refs_1_, f32[128,512]{1,0:T(8,128)} %get-tuple-element.14.refs_2_, ...), custom_call_target="tpu_custom_call" | custom-call | tf_op jit(solution)/shard_map/store_results/pallas_call | solution.py:476

commit v3 on v2

--- a/solution.py
+++ b/solution.py
@@ -12,6 +12,8 @@
 EPS = 1e-05
 NY = 4
 PARTS = 4
+SLICES = 6
+Z_GROUPS = 2
 
 f32 = jnp.float32
 bf16 = jnp.bfloat16
@@ -81,7 +83,7 @@
         probs[m, g] = jnp.where(i < count, full, 0.0)
 
 
-def attend(m, g, incoming, q, kvb, probs, both):
+def attend(m, g, incoming, q, kvb, probs, zgrads, ygrads):
     n_rows, width = q.shape[1], q.shape[2]
     per_group = width // HD // KVH
     kv_cols = KVH * HD
@@ -92,16 +94,21 @@
     p = probs[m, g]
     prob_grad = dot_t(values, head_grad)
     score_grad = p * (prob_grad - jnp.sum(p * prob_grad, axis=0, keepdims=True)) * (HD**-0.5)
-    both[rows, kv_cols + g * HD : kv_cols + (g + 1) * HD] = dot(p.astype(bf16), head_grad).astype(bf16)
-    both[rows, g * HD : (g + 1) * HD] = dot(score_grad.astype(bf16), queries).astype(bf16)
+    key_grad = dot(score_grad.astype(bf16), queries).astype(bf16)
+    first = (KVH - Z_GROUPS + g) * HD
+    ygrads[rows, first : first + HD] = dot(p.astype(bf16), head_grad).astype(bf16)
+    if g < Z_GROUPS:
+        zgrads[rows, g * HD : (g + 1) * HD] = key_grad
+    else:
+        ygrads[rows, (g - Z_GROUPS) * HD : (g - Z_GROUPS + 1) * HD] = key_grad
 
 
 def kernel(
     ns, nz, x_in, q_in, gain_in, kw_in, vw_in, cot, seg_in, counts_in,
     gout, dk, dv, gg,
-    x, q, gain, kw, vw, seg, counts, inv, normed, normed_t, normed_all, kv32, kvb, probs, kwt, vwt,
-    gin, gnext, grads, gacc, gain_y, gain_zs, gain_zr, ring_s, ring_r,
-    x_sem, q_sem, gain_sem, seg_sem, counts_sem, w_sem, cot_sem, next_s, next_r, out_sem, nt_s, nt_r, nt_l, kv_s, kv_r, gy_s, gy_r, gz_s, gz_r, ring_ss, ring_rs,
+    x, q, gain, kw, vw, seg, counts, inv, normed, normed_y, all_y, normed_z, all_z, kv32, kvb, probs, kwt, vwt,
+    gin, gnext, zgrads, ygrads, gacc, gain_y, gain_zs, gain_zr, pieces, ring_s, ring_r, key_s, key_r,
+    x_sem, q_sem, gain_sem, seg_sem, counts_sem, w_sem, cot_sem, next_s, next_r, out_sem, ny_s, ny_r, ny_l, nz_s, nz_r, nz_l, gy2_s, gy2_r, gz2_s, gz2_r, ks_s, ks_r, gy_s, gy_r, gz_s, gz_r, ring_ss, ring_rs,
 ):
     micros, n_rows, width = q.shape
     parts = w_sem.shape[1]
@@ -130,6 +137,7 @@
 
     y_peers = [device(z, along_y(k)) for k in range(1, NY)]
     up, down = device(along_z(1), y), device(along_z(-1), y)
+    z_peers = [device(along_z(k), y) for k in range(1, nz)]
     flips = [device(flipped(1 << i), y) for i in range(stages)]
 
     def remote(src, dst, ssem, rsem, dev):
@@ -158,20 +166,17 @@
 
     barrier = pltpu.get_barrier_semaphore()
     above, below = (lax.rem(sec + 1, ns), dp), (lax.rem(sec + ns - 1, ns), dp)
-    greeted = y_peers + [up, down] + flips[1:] + [above, below]
+    greeted = y_peers + z_peers + [above, below]
     for peer in greeted:
         pl.semaphore_signal(barrier, inc=1, device_id=peer, device_id_type=MESH)
 
-    def cot_copy(m, g):
-        return pltpu.make_async_copy(
-            cot.at[m, :, pl.ds(g * chunk, chunk)], gin.at[1, m, g], cot_sem.at[m, g]
-        )
+    def cot_copy(g):
+        return pltpu.make_async_copy(cot.at[:, :, pl.ds(g * chunk, chunk)], gin.at[1, :, g], cot_sem.at[g])
 
     @pl.when(is_last)
     def _():
-        for m in range(micros):
-            for g in range(KVH):
-                cot_copy(m, g).start()
+        for g in range(KVH):
+            cot_copy(g).start()
 
     kv32[...] = jnp.zeros_like(kv32)
     gacc[...] = jnp.zeros_like(gacc)
@@ -198,70 +203,81 @@
     def turn(b, carry):
         first = b * 128
         owner = lax.div(first, feats)
-        at = lax.div(owner, NY) * feats + lax.rem(first, feats)
-        normed_t[lax.rem(owner, NY), pl.ds(pl.multiple_of(at, 128), 128), :] = normed[:, aligned(b, 128)].T
+        oz, oy, offset = lax.div(owner, NY), lax.rem(owner, NY), lax.rem(first, feats)
+        block = normed[:, aligned(b, 128)].T
+        normed_y[oy, pl.ds(pl.multiple_of(oz * feats + offset, 128), 128), :] = block
+        normed_z[oz, pl.ds(pl.multiple_of(oy * feats + offset, 128), 128), :] = block
         return carry
 
     pl.semaphore_wait(barrier, len(greeted))
 
-    def nt_copy(k):
-        return remote(
-            normed_t.at[along_y(k)], normed_all.at[:, pl.ds(k * total, total)], nt_s.at[k], nt_r.at[k], y_peers[k - 1]
-        )
-
-    own_nt = pltpu.make_async_copy(normed_t.at[y], normed_all.at[:, pl.ds(0, total)], nt_l)
+    def ny_copy(k):
+        return remote(normed_y.at[along_y(k)], all_y.at[:, pl.ds(k * total, total)], ny_s.at[k], ny_r.at[k], y_peers[k - 1])
+
+    def nz_copy(k):
+        return remote(normed_z.at[along_z(k)], all_z.at[:, pl.ds(k * total, total)], nz_s.at[k], nz_r.at[k], z_peers[k - 1])
+
+    own_ny = pltpu.make_async_copy(normed_y.at[y], all_y.at[:, pl.ds(0, total)], ny_l)
+    own_nz = pltpu.make_async_copy(normed_z.at[z], all_z.at[:, pl.ds(0, total)], nz_l)
 
     def exchange_normed():
         lax.fori_loop(0, width // 128, turn, 0)
         for k in range(1, NY):
-            nt_copy(k).start()
-        own_nt.start()
+            ny_copy(k).start()
+        for k in range(1, nz):
+            nz_copy(k).start()
+        own_ny.start()
+        own_nz.start()
 
     def next_copy(m, g):
         return remote(gnext.at[m, g], gin.at[0, m, g], next_s.at[m, g], next_r.at[m, g], below)
 
-    def out_copy(m, g):
-        return pltpu.make_async_copy(
-            gnext.at[m, g], gout.at[m, :, pl.ds(g * chunk, chunk)], out_sem.at[m, g]
-        )
-
-    def kv_copy(m, k):
-        rows = aligned(m, n_rows)
-        to = pl.ds(pl.multiple_of(k * total + m * n_rows, n_rows), n_rows)
-        return remote(grads.at[rows, :], grads.at[to, :], kv_s.at[k, m], kv_r.at[k, m], y_peers[k - 1])
+    def out_copy(g):
+        return pltpu.make_async_copy(gnext.at[:, g], gout.at[:, :, pl.ds(g * chunk, chunk)], out_sem.at[g])
+
+    def rows_of(m, k):
+        return pl.ds(pl.multiple_of(k * total + m * n_rows, n_rows), n_rows)
+
+    def yg_copy(m, k):
+        return remote(ygrads.at[rows_of(m, 0), :], ygrads.at[rows_of(m, k), :], gy2_s.at[k, m], gy2_r.at[k, m], y_peers[k - 1])
+
+    def zg_copy(m, k):
+        return remote(zgrads.at[rows_of(m, 0), :], zgrads.at[rows_of(m, k), :], gz2_s.at[k, m], gz2_r.at[k, m], z_peers[k - 1])
 
     def layer(last, m, carry):
         incoming = gin.at[int(last)]
         if last:
             probabilities(m, q, kvb, seg, counts, probs)
         for g in range(KVH):
-            if last:
-                cot_copy(m, g).wait()
-            else:
+            if not last:
                 next_copy(m, g).wait_recv()
-            attend(m, g, incoming[m, g], q, kvb, probs, grads)
-        for k in range(1, NY):
-            kv_copy(m, k).start()
+            attend(m, g, incoming[m, g], q, kvb, probs, zgrads, ygrads)
         rows = aligned(m, n_rows)
-        both = grads[rows, :]
+        split = kv_cols - Z_GROUPS * HD
+        kg = jnp.concatenate([zgrads[rows, :], ygrads[rows, :split]], axis=1)
+        vg = ygrads[rows, split:]
         scale = inv[rows, 0:1]
-        pulled = jnp.sum(both.astype(f32) * kv32[rows, :], axis=1, keepdims=True) * (
-            scale * scale * (1.0 / width)
-        )
+        along = kg.astype(f32) * kv32[rows, :kv_cols] + vg.astype(f32) * kv32[rows, kv_cols:]
+        pulled = jnp.sum(along, axis=1, keepdims=True) * (scale * scale * (1.0 / width))
         for g in range(KVH):
             cols = slice(g * chunk, (g + 1) * chunk)
-            grad = (dot(both[:, :kv_cols], kwt[:, cols]) + dot(both[:, kv_cols:], vwt[:, cols])) * scale
+            grad = (dot(kg, kwt[:, cols]) + dot(vg, vwt[:, cols])) * scale
             xb = x[rows, cols].astype(f32)
             gnext[m, g] = (incoming[m, g].astype(f32) + grad * gain[:, cols] - xb * pulled).astype(bf16)
             next_copy(m, g).start()
+            if g == 0:
+                for k in range(1, NY):
+                    yg_copy(m, k).start()
+                for k in range(1, nz):
+                    zg_copy(m, k).start()
             term = grad * xb
             gacc[:, cols] += term[0:8] + term[8:16] + term[16:24] + term[24:32]
-        for g in range(KVH):
-            out_copy(m, g).start()
         return carry
 
     @pl.when(is_last)
     def _():
+        for g in range(KVH):
+            cot_copy(g).wait()
         lax.fori_loop(0, micros, functools.partial(layer, True), 0)
         exchange_normed()
 
@@ -270,6 +286,9 @@
         lax.fori_loop(0, micros, each_probs, 0)
         exchange_normed()
         lax.fori_loop(0, micros, functools.partial(layer, False), 0)
+
+    for g in range(KVH):
+        out_copy(g).start()
 
     part = width // 8
     gsum = jnp.sum(gacc[...], axis=0, keepdims=True)
@@ -302,19 +321,45 @@
             for r in range(8):
                 gg[:, r * part : (r + 1) * part] = summed[r : r + 1, :]
 
-    own_nt.wait()
+    own_ny.wait()
     for k in range(1, NY):
-        nt_copy(k).wait_recv()
-
-    def kv_waits(m, _):
+        ny_copy(k).wait_recv()
+
+    def yg_waits(m, carry):
         for k in range(1, NY):
-            kv_copy(m, k).wait_recv()
-        return _
-
-    lax.fori_loop(0, micros, kv_waits, 0)
-
-    def piece(zz, h):
-        return dot(normed_all[aligned(zz, feats), :], grads[:, h * kv_cols : (h + 1) * kv_cols])
+            yg_copy(m, k).wait_recv()
+        return carry
+
+    lax.fori_loop(0, micros, yg_waits, 0)
+    slice_cols = ygrads.shape[1] // SLICES
+
+    def each_piece(k, carry):
+        pieces[k] = dot(all_y[aligned(along_z(k), feats), :], ygrads[...])
+        return carry
+
+    def piece(k, h):
+        return pieces[k % nz, :, h * slice_cols : (h + 1) * slice_cols]
+
+    def key_piece(yy):
+        return dot(all_z[aligned(yy, feats), :], zgrads[...])
+
+    def key_copy(k):
+        return remote(key_s.at[k], key_r.at[k], ks_s.at[k], ks_r.at[k], y_peers[k - 1])
+
+    def zg_waits(m, carry):
+        for k in range(1, nz):
+            zg_copy(m, k).wait_recv()
+        return carry
+
+    def key_send():
+        own_nz.wait()
+        for k in range(1, nz):
+            nz_copy(k).wait_recv()
+        lax.fori_loop(0, micros, zg_waits, 0)
+        for k in range(1, NY):
+            key_s[k] = key_piece(along_y(k)).astype(bf16)
+            key_copy(k).start()
+        dk[:, : Z_GROUPS * HD] = key_piece(y)
 
     def ring_copy(way, t, h):
         return remote(
@@ -322,46 +367,59 @@
             (down, up)[way],
         )
 
+    def in_ring(way, t, h):
+        return t > 0 or (t == 0 and h * 2 // SLICES == way)
+
+    each_piece(half, 0)
     for t in range(half):
-        sums = {}
-        for way in range(2):
-            target = along_z((t - half) if way == 0 else (half - t))
-            for h in range(2):
-                if t > 0 or h == way:
-                    sums[way, h] = piece(target, h)
-        for h in range(2):
+        for h in range(SLICES):
             for way in range(2):
-                if (way, h) in sums:
-                    value = sums[way, h]
-                    if t > 1 or (t == 1 and h == way):
+                if in_ring(way, t, h):
+                    value = piece((t - half) if way == 0 else (half - t), h)
+                    if in_ring(way, t - 1, h):
                         ring_copy(way, t - 1, h).wait_recv()
                         value = value + ring_r[way, t - 1, h].astype(f32)
                     ring_s[way, t, h] = value.astype(bf16)
                     ring_copy(way, t, h).start()
+        if t == 0:
+            lax.fori_loop(1, half, each_piece, 0)
+            lax.fori_loop(half + 1, nz, each_piece, 0)
+            each_piece(0, 0)
+            key_send()
         if t <= stages:
             gain_stage(t)
     for t in range(half, stages + 1):
         gain_stage(t)
-    own = [piece(z, h) for h in range(2)]
-    for h, out in enumerate((dk, dv)):
-        value = own[h]
+    for h in range(SLICES):
+        value = piece(0, h)
         for way in range(2):
             ring_copy(way, half - 1, h).wait_recv()
             value = value + ring_r[way, half - 1, h].astype(f32)
-        out[...] = value
+        first = Z_GROUPS * HD + h * slice_cols
+        out = (dk, dv)[first // kv_cols]
+        out[:, first % kv_cols : first % kv_cols + slice_cols] = value
+    for k in range(1, NY):
+        key_copy(k).wait_recv()
+        dk[:, : Z_GROUPS * HD] += key_r[k].astype(f32)
 
     def sent(m, carry):
         for g in range(KVH):
             next_copy(m, g).wait_send()
-            out_copy(m, g).wait()
         for k in range(1, NY):
-            kv_copy(m, k).wait_send()
-        return carry
-
+            yg_copy(m, k).wait_send()
+        for k in range(1, nz):
+            zg_copy(m, k).wait_send()
+        return carry
+
+    for g in range(KVH):
+        out_copy(g).wait()
     lax.fori_loop(0, micros, sent, 0)
     for k in range(1, NY):
-        nt_copy(k).wait_send()
+        ny_copy(k).wait_send()
         gy_copy(k).wait_send()
+        key_copy(k).wait_send()
+    for k in range(1, nz):
+        nz_copy(k).wait_send()
 
     @pl.when(is_last)
     def _():
@@ -373,8 +431,8 @@
         gz_copy(i).wait_send()
     for t in range(half):
         for way in range(2):
-            for h in range(2):
-                if t > 0 or h == way:
+            for h in range(SLICES):
+                if in_ring(way, t, h):
                     ring_copy(way, t, h).wait_send()
 
 
@@ -397,6 +455,8 @@
     feats = width // nd
     half = nz // 2
     stages = nz.bit_length() - 1
+    z_cols = Z_GROUPS * HD
+    y_cols = 2 * kv_cols - z_cols
     vmem = pl.BlockSpec(memory_space=pltpu.VMEM)
     hbm = pl.BlockSpec(memory_space=pltpu.HBM)
     dma = pltpu.SemaphoreType.DMA
@@ -422,6 +482,8 @@
             pltpu.VMEM((total, width), bf16),
             pltpu.VMEM((NY, nz * feats, total), bf16),
             pltpu.VMEM((nz * feats, NY * total), bf16),
+            pltpu.VMEM((nz, NY * feats, total), bf16),
+            pltpu.VMEM((NY * feats, nz * total), bf16),
             pltpu.VMEM((total, 2 * kv_cols), f32),
             pltpu.VMEM((total, 2 * kv_cols), bf16),
             pltpu.VMEM((micros, KVH, n_rows, n_rows * per_group), f32),
@@ -429,34 +491,45 @@
             pltpu.VMEM((kv_cols, width), bf16),
             pltpu.VMEM((2, micros, KVH, n_rows, chunk), bf16),
             pltpu.VMEM((micros, KVH, n_rows, chunk), bf16),
-            pltpu.VMEM((NY * total, 2 * kv_cols), bf16),
+            pltpu.VMEM((nz * total, z_cols), bf16),
+            pltpu.VMEM((NY * total, y_cols), bf16),
             pltpu.VMEM((8, width), f32),
             pltpu.VMEM((NY, 8, width // 8), f32),
             pltpu.VMEM((stages, 8, width // 8), f32),
             pltpu.VMEM((stages, 8, width // 8), f32),
-            pltpu.VMEM((2, half, 2, feats, kv_cols), bf16),
-            pltpu.VMEM((2, half, 2, feats, kv_cols), bf16),
+            pltpu.VMEM((nz, feats, y_cols), f32),
+            pltpu.VMEM((2, half, SLICES, feats, y_cols // SLICES), bf16),
+            pltpu.VMEM((2, half, SLICES, feats, y_cols // SLICES), bf16),
+            pltpu.VMEM((NY, feats, z_cols), bf16),
+            pltpu.VMEM((NY, feats, z_cols), bf16),
             dma,
             dma,
             dma,
             dma,
             dma,
             dma((2, PARTS)),
+            dma((KVH,)),
             dma((micros, KVH)),
             dma((micros, KVH)),
-            dma((micros, KVH)),
-            dma((micros, KVH)),
+            dma((KVH,)),
             dma((NY,)),
             dma((NY,)),
             dma,
+            dma((nz,)),
+            dma((nz,)),
+            dma,
             dma((NY, micros)),
             dma((NY, micros)),
+            dma((nz, micros)),
+            dma((nz, micros)),
+            dma((NY,)),
+            dma((NY,)),
             dma((NY,)),
             dma((NY,)),
             dma((stages,)),
             dma((stages,)),
-            dma((2, half, 2)),
-            dma((2, half, 2)),
+            dma((2, half, SLICES)),
+            dma((2, half, SLICES)),
         ],
         compiler_params=pltpu.CompilerParams(
             collective_id=0, has_side_effects=True, vmem_limit_bytes=60 * 2**20

time: 90.1 us -> 84.9 us (0.942)
  Pallas kernels: 89.3 us -> 84.1 us
    pallas_call x1, Pallas kernels: 86.8 us -> 81.6 us  [shards(): pl.pallas_call(functools.partial(kernel, ns, nz), out_shape=(jax.ShapeDty...]
where the time goes in v3:
time: 84.9 us; the launch traced here: 84.8 us
  Pallas kernels  84.1 us (99%)
    pallas_call x1, Pallas kernels, shards(): pl.pallas_call(functools.partial(kernel, ns, nz), out_shape=(jax.ShapeDty...  81.6 us
    pallas_call x1, Pallas kernels, shards(): pl.pallas_call(store, out_shape=tuple((jax.ShapeDtypeStruct(r.shape, r.dt...  2.52 us

profile of v3, /device:TPU:32, one launch (start us, length us, event | category | flops | bytes accessed | tf_op | source)
XLA Modules:
  0.0 84.8 jit_solution(1100005607311744618)
XLA Ops:
  0.6 81.6 %layers_backward.1 = (bf16[4,32,4096]{2,1,0:T(8,128)(2,1)}, f32[128,512]{1,0:T(8,128)}, f32[128,512]{1,0:T(8,128)}, f32[1,4096]{1,0:T(1,128)}) custom-call(bf16[128,4096]{1,0:T(8,128)(2,1)} %bitcast.11, bf16[4,32,4096]{2,1,0:T(8,128)(2,1)} %bitcast.12, f32[1,4096]{1,0:T(1,128)} %gain_in.1, bf16[4096,512]{1,0:T(8,128)(2,1)} %bitcast.9, ...), custom_call_target="tpu_custom_call" | custom-call | tf_op jit(solution)/shard_map/layers_backward/pallas_call | solution.py:463
  82.2 2.5 %store_results.1 = (bf16[4,32,4096]{2,1,0:T(8,128)(2,1)}, f32[128,512]{1,0:T(8,128)}, f32[128,512]{1,0:T(8,128)}, f32[1,4096]{1,0:T(1,128)}) custom-call(bf16[4,32,4096]{2,1,0:T(8,128)(2,1)} %get-tuple-element.12.refs_0_, f32[128,512]{1,0:T(8,128)} %get-tuple-element.13.refs_1_, f32[128,512]{1,0:T(8,128)} %get-tuple-element.14.refs_2_, ...), custom_call_target="tpu_custom_call" | custom-call | tf_op jit(solution)/shard_map/store_results/pallas_call | solution.py:549

commit v4 on v3

--- a/solution.py
+++ b/solution.py
@@ -11,7 +11,7 @@
 KVH = 4
 EPS = 1e-05
 NY = 4
-PARTS = 4
+PARTS = 2
 SLICES = 6
 Z_GROUPS = 2
 
@@ -105,10 +105,10 @@
 
 def kernel(
     ns, nz, x_in, q_in, gain_in, kw_in, vw_in, cot, seg_in, counts_in,
-    gout, dk, dv, gg,
+    gout, dk_out, dv_out, gg_out, dk, dv, gg,
     x, q, gain, kw, vw, seg, counts, inv, normed, normed_y, all_y, normed_z, all_z, kv32, kvb, probs, kwt, vwt,
     gin, gnext, zgrads, ygrads, gacc, gain_y, gain_zs, gain_zr, pieces, ring_s, ring_r, key_s, key_r,
-    x_sem, q_sem, gain_sem, seg_sem, counts_sem, w_sem, cot_sem, next_s, next_r, out_sem, ny_s, ny_r, ny_l, nz_s, nz_r, nz_l, gy2_s, gy2_r, gz2_s, gz2_r, ks_s, ks_r, gy_s, gy_r, gz_s, gz_r, ring_ss, ring_rs,
+    x_sem, q_sem, gain_sem, seg_sem, counts_sem, w_sem, cot_sem, next_s, next_r, out_sem, ny_s, ny_r, ny_l, nz_s, nz_r, nz_l, gy2_s, gy2_r, gz2_s, gz2_r, ks_s, ks_r, gy_s, gy_r, gz_s, gz_r, ring_ss, ring_rs, slice_sem, key_sem, gg_sem,
 ):
     micros, n_rows, width = q.shape
     parts = w_sem.shape[1]
@@ -156,33 +156,33 @@
     counts_copy = pltpu.make_async_copy(counts_in, counts, counts_sem)
     x_copy.start()
     gain_copy.start()
-    for c in range(parts):
-        for p in range(2):
-            w_copy(p, c).start()
-        if c == 0:
-            q_copy.start()
-            seg_copy.start()
-            counts_copy.start()
-
     barrier = pltpu.get_barrier_semaphore()
     above, below = (lax.rem(sec + 1, ns), dp), (lax.rem(sec + ns - 1, ns), dp)
     greeted = y_peers + z_peers + [above, below]
     for peer in greeted:
         pl.semaphore_signal(barrier, inc=1, device_id=peer, device_id_type=MESH)
 
+    for c in range(parts):
+        for p in range(2):
+            w_copy(p, c).start()
+
     def cot_copy(g):
         return pltpu.make_async_copy(cot.at[:, :, pl.ds(g * chunk, chunk)], gin.at[1, :, g], cot_sem.at[g])
+
+    kv32[...] = jnp.zeros_like(kv32)
+    gacc[...] = jnp.zeros_like(gacc)
+    x_copy.wait()
+    gain_copy.wait()
+    q_copy.start()
+    seg_copy.start()
+    counts_copy.start()
+    normalise(x, gain, inv, normed)
 
     @pl.when(is_last)
     def _():
         for g in range(KVH):
             cot_copy(g).start()
 
-    kv32[...] = jnp.zeros_like(kv32)
-    gacc[...] = jnp.zeros_like(gacc)
-    x_copy.wait()
-    gain_copy.wait()
-    normalise(x, gain, inv, normed)
 
     def each_part(c, carry):
         for p in range(2):
@@ -243,6 +243,12 @@
 
     def zg_copy(m, k):
         return remote(zgrads.at[rows_of(m, 0), :], zgrads.at[rows_of(m, k), :], gz2_s.at[k, m], gz2_r.at[k, m], z_peers[k - 1])
+
+    def send_grads(m):
+        for k in range(1, NY):
+            yg_copy(m, k).start()
+        for k in range(1, nz):
+            zg_copy(m, k).start()
 
     def layer(last, m, carry):
         incoming = gin.at[int(last)]
@@ -253,6 +259,7 @@
                 next_copy(m, g).wait_recv()
             attend(m, g, incoming[m, g], q, kvb, probs, zgrads, ygrads)
         rows = aligned(m, n_rows)
+        pl.when(m == micros - 1)(functools.partial(send_grads, m))
         split = kv_cols - Z_GROUPS * HD
         kg = jnp.concatenate([zgrads[rows, :], ygrads[rows, :split]], axis=1)
         vg = ygrads[rows, split:]
@@ -266,10 +273,7 @@
             gnext[m, g] = (incoming[m, g].astype(f32) + grad * gain[:, cols] - xb * pulled).astype(bf16)
             next_copy(m, g).start()
             if g == 0:
-                for k in range(1, NY):
-                    yg_copy(m, k).start()
-                for k in range(1, nz):
-                    zg_copy(m, k).start()
+                pl.when(m < micros - 1)(functools.partial(send_grads, m))
             term = grad * xb
             gacc[:, cols] += term[0:8] + term[8:16] + term[16:24] + term[24:32]
         return carry
@@ -390,6 +394,20 @@
             gain_stage(t)
     for t in range(half, stages + 1):
         gain_stage(t)
+    def result_copy(h):
+        first = Z_GROUPS * HD + h * slice_cols
+        cols = pl.ds(first % kv_cols, slice_cols)
+        buf, out = ((dk, dk_out), (dv, dv_out))[first // kv_cols]
+        return pltpu.make_async_copy(buf.at[:, cols], out.at[:, cols], slice_sem.at[h])
+
+    z_part = pl.ds(0, Z_GROUPS * HD)
+    key_out = pltpu.make_async_copy(dk.at[:, z_part], dk_out.at[:, z_part], key_sem)
+    gg_copy = pltpu.make_async_copy(gg, gg_out, gg_sem)
+    gg_copy.start()
+    for k in range(1, NY):
+        key_copy(k).wait_recv()
+        dk[:, : Z_GROUPS * HD] += key_r[k].astype(f32)
+    key_out.start()
     for h in range(SLICES):
         value = piece(0, h)
         for way in range(2):
@@ -398,10 +416,12 @@
         first = Z_GROUPS * HD + h * slice_cols
         out = (dk, dv)[first // kv_cols]
         out[:, first % kv_cols : first % kv_cols + slice_cols] = value
-    for k in range(1, NY):
-        key_copy(k).wait_recv()
-        dk[:, : Z_GROUPS * HD] += key_r[k].astype(f32)
-
+        result_copy(h).start()
+
+    gg_copy.wait()
+    key_out.wait()
+    for h in range(SLICES):
+        result_copy(h).wait()
     def sent(m, carry):
         for g in range(KVH):
             next_copy(m, g).wait_send()
@@ -436,12 +456,18 @@
                     ring_copy(way, t, h).wait_send()
 
 
-def store(*refs):
-    count = len(refs) // 2
-    copies = [pltpu.make_async_copy(refs[r], refs[count + r], refs[-1].at[r]) for r in range(count)]
-    for copy in copies:
+def store(gout, dk, dv, gg, gout_to, dk_to, dv_to, gg_to, *held):
+    sems = held[-1]
+    parts = [(gout.at[m], gout_to.at[m], held[0].at[m]) for m in range(gout.shape[0])]
+    parts = [(dk, dk_to, held[1]), (dv, dv_to, held[2]), (gg, gg_to, held[3])] + parts
+    loads = [pltpu.make_async_copy(src, buf, sems.at[0, r]) for r, (src, _, buf) in enumerate(parts)]
+    stores = [pltpu.make_async_copy(buf, dst, sems.at[1, r]) for r, (_, dst, buf) in enumerate(parts)]
+    for copy in loads:
         copy.start()
-    for copy in copies:
+    for r in range(len(parts)):
+        loads[r].wait()
+        stores[r].start()
+    for copy in stores:
         copy.wait()
 
 
@@ -469,8 +495,11 @@
             jax.ShapeDtypeStruct((1, width), f32),
         ),
         in_specs=[hbm] * 8,
-        out_specs=(hbm, vmem, vmem, vmem),
+        out_specs=(hbm, hbm, hbm, hbm),
         scratch_shapes=[
+            pltpu.VMEM((feats, kv_cols), f32),
+            pltpu.VMEM((feats, kv_cols), f32),
+            pltpu.VMEM((1, width), f32),
             pltpu.VMEM((total, width), bf16),
             pltpu.VMEM((micros, n_rows, width), bf16),
             pltpu.VMEM((1, width), f32),
@@ -530,6 +559,9 @@
             dma((stages,)),
             dma((2, half, SLICES)),
             dma((2, half, SLICES)),
+            dma((SLICES,)),
+            dma,
+            dma,
         ],
         compiler_params=pltpu.CompilerParams(
             collective_id=0, has_side_effects=True, vmem_limit_bytes=60 * 2**20
@@ -549,9 +581,9 @@
     gout, dk, dv, gg = pl.pallas_call(
         store,
         out_shape=tuple(jax.ShapeDtypeStruct(r.shape, r.dtype) for r in results),
-        in_specs=[vmem] * len(results),
+        in_specs=[hbm] * len(results),
         out_specs=(hbm,) * len(results),
-        scratch_shapes=[dma((len(results),))],
+        scratch_shapes=[pltpu.VMEM(r.shape, r.dtype) for r in results] + [dma((2, micros + 3))],
         compiler_params=pltpu.CompilerParams(vmem_limit_bytes=60 * 2**20),
         name="store_results",
     )(*results)

time: 84.9 us -> 82 us (0.966)
  Pallas kernels: 84.1 us -> 81.2 us
    pallas_call x1, Pallas kernels: 81.6 us -> 79 us  [shards(): pl.pallas_call(functools.partial(kernel, ns, nz), out_shape=(jax.ShapeDty...]
where the time goes in v4:
time: 82 us; the launch traced here: 81.9 us
  Pallas kernels  81.2 us (99%)
    pallas_call x1, Pallas kernels, shards(): pl.pallas_call(functools.partial(kernel, ns, nz), out_shape=(jax.ShapeDty...  79 us
    pallas_call x1, Pallas kernels, shards(): pl.pallas_call(store, out_shape=tuple((jax.ShapeDtypeStruct(r.shape, r.dt...  2.21 us

profile of v4, /device:TPU:32, one launch (start us, length us, event | category | flops | bytes accessed | tf_op | source)
XLA Modules:
  0.0 81.9 jit_solution(16943587587194493)
XLA Ops:
  0.6 79.0 %layers_backward.1 = (bf16[4,32,4096]{2,1,0:T(8,128)(2,1)}, f32[128,512]{1,0:T(8,128)}, f32[128,512]{1,0:T(8,128)}, f32[1,4096]{1,0:T(1,128)}) custom-call(bf16[128,4096]{1,0:T(8,128)(2,1)} %bitcast.11, bf16[4,32,4096]{2,1,0:T(8,128)(2,1)} %bitcast.12, f32[1,4096]{1,0:T(1,128)} %gain_in.1, bf16[4096,512]{1,0:T(8,128)(2,1)} %bitcast.9, ...), custom_call_target="tpu_custom_call" | custom-call | tf_op jit(solution)/shard_map/layers_backward/pallas_call | solution.py:489
  79.7 2.2 %store_results.1 = (bf16[4,32,4096]{2,1,0:T(8,128)(2,1)}, f32[128,512]{1,0:T(8,128)}, f32[128,512]{1,0:T(8,128)}, f32[1,4096]{1,0:T(1,128)}) custom-call(bf16[4,32,4096]{2,1,0:T(8,128)(2,1)} %get-tuple-element.12.gout, f32[128,512]{1,0:T(8,128)} %get-tuple-element.13.dk, f32[128,512]{1,0:T(8,128)} %get-tuple-element.14.dv, f32[1,4096]{1,0:T(1,128)} %get-tuple-element.15.gg), custom_call_target="tpu_custom_call" | custom-call | tf_op jit(solution)/shard_map/store_results/pallas_call | solution.py:581

commit v5 on v4

--- a/solution.py
+++ b/solution.py
@@ -247,7 +247,7 @@
     def send_grads(m):
         for k in range(1, NY):
             yg_copy(m, k).start()
-        for k in range(1, nz):
+        for k in sorted(range(1, nz), key=lambda k: -min(k, nz - k)):
             zg_copy(m, k).start()
 
     def layer(last, m, carry):
@@ -389,6 +389,7 @@
             lax.fori_loop(1, half, each_piece, 0)
             lax.fori_loop(half + 1, nz, each_piece, 0)
             each_piece(0, 0)
+        if t == min(1, half - 1):
             key_send()
         if t <= stages:
             gain_stage(t)

time: 82 us -> 82 us (level)
  no operation moved by 1% of the time
where the time goes in v5:
time: 82 us; the launch traced here: 81.8 us
  Pallas kernels  81.2 us (99%)
    pallas_call x1, Pallas kernels, shards(): pl.pallas_call(functools.partial(kernel, ns, nz), out_shape=(jax.ShapeDty...  79 us
    pallas_call x1, Pallas kernels, shards(): pl.pallas_call(store, out_shape=tuple((jax.ShapeDtypeStruct(r.shape, r.dt...  2.21 us

profile of v5, /device:TPU:32, one launch (start us, length us, event | category | flops | bytes accessed | tf_op | source)
XLA Modules:
  0.0 81.8 jit_solution(5278047833367059047)
XLA Ops:
  0.6 79.0 %layers_backward.1 = (bf16[4,32,4096]{2,1,0:T(8,128)(2,1)}, f32[128,512]{1,0:T(8,128)}, f32[128,512]{1,0:T(8,128)}, f32[1,4096]{1,0:T(1,128)}) custom-call(bf16[128,4096]{1,0:T(8,128)(2,1)} %bitcast.11, bf16[4,32,4096]{2,1,0:T(8,128)(2,1)} %bitcast.12, f32[1,4096]{1,0:T(1,128)} %gain_in.1, bf16[4096,512]{1,0:T(8,128)(2,1)} %bitcast.9, ...), custom_call_target="tpu_custom_call" | custom-call | tf_op jit(solution)/shard_map/layers_backward/pallas_call | solution.py:490
  79.6 2.2 %store_results.1 = (bf16[4,32,4096]{2,1,0:T(8,128)(2,1)}, f32[128,512]{1,0:T(8,128)}, f32[128,512]{1,0:T(8,128)}, f32[1,4096]{1,0:T(1,128)}) custom-call(bf16[4,32,4096]{2,1,0:T(8,128)(2,1)} %get-tuple-element.12.gout, f32[128,512]{1,0:T(8,128)} %get-tuple-element.13.dk, f32[128,512]{1,0:T(8,128)} %get-tuple-element.14.dv, f32[1,4096]{1,0:T(1,128)} %get-tuple-element.15.gg), custom_call_target="tpu_custom_call" | custom-call | tf_op jit(solution)/shard_map/store_results/pallas_call | solution.py:582
